TPU v7x, 512 devices: a whole 4x8x8 slice. The times are simulated.
512 devices in a mesh: ens: 16 (over y, core), lat: 32 (over x, z).
Axes of the slice: x: 4, y: 8, z: 8, core: 2. Of those that a mesh axis runs over, the one named last changes fastest.
Arguments:
- members: bfloat16 [16, 64, 384, 720], P('ens', None, 'lat'), may hold values from -6 to 6
- analysis: bfloat16 [64, 384, 720], P(None, 'lat'), may hold values from -6 to 6
- wave_order: int32 [320], replicated, may hold values from 0 to 319, each once
Outputs:
- grid_grad: bfloat16 [16, 64, 384, 720], P('ens', None, 'lat')
- coef_score: float32 [320, 320], P('lat', 'ens')
Inputs may be any that keep to these rules, and one draw needn't show every extreme that they name: wave_order names each wavenumber from 0 to 319 exactly once.
All inputs are finite; a program needn't handle non-finite values.
Results may differ from a plain program's by a relative error of at most 0.014.
The roundings to bfloat16 on the way count: a program that leaves them out, or rounds other values in their place, can miss the bound.
Values may be sent and summed in bfloat16 or wider, within the bound.
No kernel may reach another device: no remote copies, remote signals or barrier semaphores. Data moves between devices by JAX's collectives and lax.ppermute only.
A program may use at most 128 MiB of HBM per device.

v0:
```python
import math

import jax
import jax.numpy as jnp
from jax import lax
from jax.sharding import PartitionSpec as P

SOFTNESS = 0.1
CEILING = 2.0**60
SHRINK = 2.0 ** (-60)
LOG_SHIFT = 60.0 * math.log(2.0)
degree_block = 32


def fourier_table(wave_order, count_lon):
    lon_index = jnp.arange(count_lon, dtype=jnp.int32)
    product = lon_index[:, None] * wave_order[None, :] % count_lon
    angle = 2.0 * math.pi / count_lon * product.astype(jnp.float32)
    norm_lon = 1.0 / math.sqrt(count_lon)
    return jnp.stack([jnp.cos(angle) * norm_lon, -jnp.sin(angle) * norm_lon], axis=-1).astype(
        jnp.bfloat16
    )


def degree_step(carry, degree, wave_f, cosine, weight):
    previous, older, scale_prev, log_scale = carry
    denom = jnp.maximum(degree * degree - wave_f * wave_f, 1.0)
    factor = jnp.sqrt(jnp.maximum(4.0 * degree * degree - 1.0, 1.0) / denom)
    recurred = factor * (cosine * previous - older / scale_prev)
    current = jnp.where(degree < wave_f, 0.0, jnp.where(degree == wave_f, 1.0, recurred))
    too_large = jnp.abs(current) > CEILING
    current = jnp.where(too_large, current * SHRINK, current)
    previous = jnp.where(too_large, previous * SHRINK, previous)
    log_scale = jnp.where(too_large, log_scale + LOG_SHIFT, log_scale)
    carried = jnp.where(degree > wave_f, factor, 1.0)
    produced = (weight * (current * jnp.exp(log_scale))).astype(jnp.bfloat16)
    return ((current, previous, carried, log_scale), produced)


def legendre_rows(slot_waves, count_lat, count_degree):
    lat_index = jnp.arange(count_lat, dtype=jnp.int32).astype(jnp.float32)
    colatitude = (lat_index + 0.5) * (math.pi / count_lat)
    cosine = jnp.cos(colatitude)[None, :]
    sine_row = jnp.sin(colatitude)[None, :]
    weight = math.sqrt(math.pi / count_lat) * sine_row
    wave_f = slot_waves.astype(jnp.float32)[:, None]
    start_log = 0.5 * (
        lax.lgamma(wave_f + 1.5)
        - lax.lgamma(wave_f + 1.0)
        - lax.lgamma(jnp.float32(1.5))
        + math.log(0.5)
    ) + wave_f * jnp.log(sine_row)
    zero_rows = jnp.zeros((slot_waves.shape[0], count_lat), jnp.float32)
    initial = (zero_rows, zero_rows, jnp.ones((slot_waves.shape[0], 1), jnp.float32), start_log)

    def block_step(carry, first_degree):
        emitted = []
        for offset in range(degree_block):
            degree = (first_degree + offset).astype(jnp.float32)
            carry, produced = degree_step(carry, degree, wave_f, cosine, weight)
            emitted.append(produced)
        return (carry, jnp.stack(emitted))

    starts = jnp.arange(count_degree // degree_block, dtype=jnp.int32) * degree_block
    _, rows_out = lax.scan(block_step, initial, starts)
    return rows_out.reshape(count_degree, slot_waves.shape[0], count_lat)


def crps_terms(spectra):
    count_members = spectra.shape[0]
    smooth_abs = jnp.sqrt(spectra * spectra + SOFTNESS * SOFTNESS)
    pair_diff = spectra[:, None] - spectra[None, :]
    pair_abs = jnp.sqrt(pair_diff * pair_diff + SOFTNESS * SOFTNESS)
    coef_grad = spectra / smooth_abs - jnp.sum(pair_diff / pair_abs, axis=1) / (count_members - 1)
    per_coef = jnp.sum(smooth_abs - SOFTNESS, axis=0) / count_members - jnp.sum(
        pair_abs - SOFTNESS, axis=(0, 1)
    ) / (2 * count_members * (count_members - 1))
    return (coef_grad, jnp.sum(per_coef, axis=(-2, -1)))


def inverse_fourier(received, table_full):
    return jnp.einsum(
        "sjpv,ksp->vjk", received, table_full, preferred_element_type=jnp.float32
    ).astype(jnp.bfloat16)


def body(members, analysis, wave_order):
    deviation = (members[0].astype(jnp.float32) - analysis.astype(jnp.float32)).astype(jnp.bfloat16)
    table_full = fourier_table(wave_order, deviation.shape[2])
    fourier = jnp.einsum(
        "vjk,ksp->sjpv", deviation, table_full, preferred_element_type=jnp.float32
    ).astype(jnp.bfloat16)
    degree_count = wave_order.shape[0]
    slot_count = degree_count // lax.axis_size("lat")
    slot_waves = lax.dynamic_slice_in_dim(
        wave_order, lax.axis_index("lat") * slot_count, slot_count
    )
    gathered = lax.all_to_all(fourier, "lat", split_axis=0, concat_axis=1, tiled=True)
    legendre = legendre_rows(slot_waves, gathered.shape[1], degree_count)
    spectra = jnp.einsum(
        "lsj,sjpv->slpv", legendre, gathered, preferred_element_type=jnp.float32
    ).astype(jnp.bfloat16)
    received = lax.all_to_all(spectra[:, None], "ens", split_axis=2, concat_axis=1, tiled=True)
    coef_grad, totals = lax.map(crps_terms, received.astype(jnp.float32))
    returned = lax.all_to_all(
        coef_grad.astype(jnp.bfloat16), "ens", split_axis=1, concat_axis=2, tiled=True
    )
    coef_grad = returned[:, 0]
    coef_score = totals / (2 * received.shape[4])
    returned = jnp.einsum(
        "lsj,slpv->sjpv", legendre, coef_grad, preferred_element_type=jnp.float32
    ).astype(jnp.bfloat16)
    grid_grad = inverse_fourier(
        lax.all_to_all(returned, "lat", split_axis=1, concat_axis=0, tiled=True), table_full
    )
    return (grid_grad[None], coef_score)


def solution(mesh):
    placed = (P("ens", None, "lat", None), P(None, "lat", None), P())
    return jax.shard_map(
        body,
        mesh=mesh,
        in_specs=placed,
        out_specs=(P("ens", None, "lat", None), P("lat", "ens")),
        check_vma=False,
    )
```

profile of v0, /device:TPU:1, one launch (start us, length us, event | category | flops | bytes accessed | tf_op | source)
XLA Modules:
  0.0 517.1 jit_solution(9097416078344853190)
XLA Ops:
  0.6 5.6 %multiply_convert_fusion.33 = (bf16[720,320,1]{0,1,2:T(8,128)(2,1)S(1)}, bf16[720,320,1]{0,1,2:T(8,128)(2,1)S(1)}) fusion(s32[320]{0:T(512)} %param.9), kind=kLoop, calls=%fused_computation.539 | loop fusion | flops 3225600 | bytes 922880 | tf_op jit(solution)/shard_map/convert.2
  7.2 2.8 fusion.194
  10.0 1.9 copy.85
  11.9 2.0 reshape.2179
  14.0 13.7 %all-to-all-start = ((bf16[32,2,7680]{2,1,0:T(2,128)(2,1)}), bf16[32,2,7680]{2,1,0:T(2,128)(2,1)S(1)}, u32[]{:S(2)}, u32[]{:S(2)}) async-start(bf16[32,2,7680]{2,1,0:T(2,128)(2,1)} %reshape.2179), calls=%async_computation | async-start | bytes 1966080 | tf_op jit(solution)/shard_map/all_to_all | solution.py:98
  28.7 272.1 %while.39 = (s32[]{:T(128)}, f32[10,384]{1,0:T(8,128)S(1)}, f32[10,384]{1,0:T(8,128)S(1)}, f32[10,1]{0,1:T(1,128)S(1)}, f32[10,384]{1,0:T(8,128)S(1)}, /*index=5...) while((s32[]{:T(128)}, f32[10,384]{1,0:T(8,128)S(1)}, ...), condition=%wide.region_1.2_spmd.clone.clone, body=%wide.region_0.1_spmd.clone.clone.sunk | while | flops 3188523 | bytes 4818829 | solution.py:65
  300.8 1.2 reshape.2180
  302.0 2.9 copy.86
  305.0 3.8 copy.88
  308.7 3.2 fusion.190
  312.1 1.6 copy.89
  313.7 1.8 reshape.2181
  315.5 8.1 %all-to-all-start.1 = ((bf16[16,2,12800]{2,1,0:T(2,128)(2,1)}), bf16[16,2,12800]{2,1,0:T(2,128)(2,1)S(1)}, u32[]{:S(2)}, u32[]{:S(2)}) async-start(bf16[16,2,12800]{2,1,0:T(2,128)(2,1)} %reshape.2181), calls=%async_computation.1 | async-start | bytes 1638400 | tf_op jit(solution)/shard_map/all_to_all | solution.py:103
  323.6 23.3 %all-to-all-done.1 = bf16[16,2,12800]{2,1,0:T(2,128)(2,1)S(1)} async-done(((bf16[16,2,12800]{2,1,0:T(2,128)(2,1)}), bf16[16,2,12800]{2,1,0:T(2,128)(2,1)S(1)}, u32[]{:S(2)}, u32[]{:S(2)}) %all-to-all-start.1) | async-done | bytes 819232 | tf_op jit(solution)/shard_map/all_to_all | solution.py:103
  347.9 3.0 copy.90
  350.9 3.4 copy.91
  354.3 80.1 %while.38 = (s32[]{:T(128)}, bf16[10,16,20,2,64]{4,3,2,0,1:T(2,128)(2,1)}, f32[10,20]{1,0:T(8,128)S(1)}, f32[10,16,20,2,64]{4,3,2,1,0:T(2,128)S(1)}, s32[]{:T(128)}, /*index=5*/s32[]{:T(128)}) while((s32[]{:T(128)}, bf16[10,16,20,2,64]{4,3,2,0,1:T(2,128)(2,1)}, f32[10,20]{1,0:T(8,128)S(1)}, f32[10,16,20,2,64]{4,3,2,1,0:T(2,128)S(1)}, ...), condition=%wide.region_7.8_spmd, body=%wide.region_2.7_spmd.sunk | while | flops 4920302 | bytes 2499389 | solution.py:104
  354.6 5.3 %fusion.252 = (f32[20,2,64]{2,1,0:T(2,128)S(1)}, f32[16,20,2,64]{3,2,1,0:T(2,128)}) fusion(f32[16,20,2,64]{3,0,2,1:T(8,128)S(1)} %bitcast.646, f32[16,20,2,64]{3,2,1,0:T(2,128)S(1)} %copy.124), kind=kLoop, calls=%fused_computation.8.clone.1 | loop fusion | flops 4544000 | bytes 501760 | tf_op jit(solution)/shard_map/while/body/eval_jaxpr/reduce_sum | solution.py:75
  360.4 2.0 bitcast_dynamic-update-slice_fusion.4
  362.7 5.3 %fusion.252 = (f32[20,2,64]{2,1,0:T(2,128)S(1)}, f32[16,20,2,64]{3,2,1,0:T(2,128)}) fusion(f32[16,20,2,64]{3,0,2,1:T(8,128)S(1)} %bitcast.646, f32[16,20,2,64]{3,2,1,0:T(2,128)S(1)} %copy.124), kind=kLoop, calls=%fused_computation.8.clone.1 | loop fusion | flops 4544000 | bytes 501760 | tf_op jit(solution)/shard_map/while/body/eval_jaxpr/reduce_sum | solution.py:75
  368.4 2.0 bitcast_dynamic-update-slice_fusion.4
  370.7 5.3 %fusion.252 = (f32[20,2,64]{2,1,0:T(2,128)S(1)}, f32[16,20,2,64]{3,2,1,0:T(2,128)}) fusion(f32[16,20,2,64]{3,0,2,1:T(8,128)S(1)} %bitcast.646, f32[16,20,2,64]{3,2,1,0:T(2,128)S(1)} %copy.124), kind=kLoop, calls=%fused_computation.8.clone.1 | loop fusion | flops 4544000 | bytes 501760 | tf_op jit(solution)/shard_map/while/body/eval_jaxpr/reduce_sum | solution.py:75
  376.4 1.9 bitcast_dynamic-update-slice_fusion.4
  378.6 5.3 %fusion.252 = (f32[20,2,64]{2,1,0:T(2,128)S(1)}, f32[16,20,2,64]{3,2,1,0:T(2,128)}) fusion(f32[16,20,2,64]{3,0,2,1:T(8,128)S(1)} %bitcast.646, f32[16,20,2,64]{3,2,1,0:T(2,128)S(1)} %copy.124), kind=kLoop, calls=%fused_computation.8.clone.1 | loop fusion | flops 4544000 | bytes 501760 | tf_op jit(solution)/shard_map/while/body/eval_jaxpr/reduce_sum | solution.py:75
  384.4 2.0 bitcast_dynamic-update-slice_fusion.4
  386.6 5.3 %fusion.252 = (f32[20,2,64]{2,1,0:T(2,128)S(1)}, f32[16,20,2,64]{3,2,1,0:T(2,128)}) fusion(f32[16,20,2,64]{3,0,2,1:T(8,128)S(1)} %bitcast.646, f32[16,20,2,64]{3,2,1,0:T(2,128)S(1)} %copy.124), kind=kLoop, calls=%fused_computation.8.clone.1 | loop fusion | flops 4544000 | bytes 501760 | tf_op jit(solution)/shard_map/while/body/eval_jaxpr/reduce_sum | solution.py:75
  392.4 2.0 bitcast_dynamic-update-slice_fusion.4
  394.6 5.3 %fusion.252 = (f32[20,2,64]{2,1,0:T(2,128)S(1)}, f32[16,20,2,64]{3,2,1,0:T(2,128)}) fusion(f32[16,20,2,64]{3,0,2,1:T(8,128)S(1)} %bitcast.646, f32[16,20,2,64]{3,2,1,0:T(2,128)S(1)} %copy.124), kind=kLoop, calls=%fused_computation.8.clone.1 | loop fusion | flops 4544000 | bytes 501760 | tf_op jit(solution)/shard_map/while/body/eval_jaxpr/reduce_sum | solution.py:75
  400.4 2.0 bitcast_dynamic-update-slice_fusion.4
  402.6 5.3 %fusion.252 = (f32[20,2,64]{2,1,0:T(2,128)S(1)}, f32[16,20,2,64]{3,2,1,0:T(2,128)}) fusion(f32[16,20,2,64]{3,0,2,1:T(8,128)S(1)} %bitcast.646, f32[16,20,2,64]{3,2,1,0:T(2,128)S(1)} %copy.124), kind=kLoop, calls=%fused_computation.8.clone.1 | loop fusion | flops 4544000 | bytes 501760 | tf_op jit(solution)/shard_map/while/body/eval_jaxpr/reduce_sum | solution.py:75
  408.4 2.0 bitcast_dynamic-update-slice_fusion.4
  410.6 5.3 %fusion.252 = (f32[20,2,64]{2,1,0:T(2,128)S(1)}, f32[16,20,2,64]{3,2,1,0:T(2,128)}) fusion(f32[16,20,2,64]{3,0,2,1:T(8,128)S(1)} %bitcast.646, f32[16,20,2,64]{3,2,1,0:T(2,128)S(1)} %copy.124), kind=kLoop, calls=%fused_computation.8.clone.1 | loop fusion | flops 4544000 | bytes 501760 | tf_op jit(solution)/shard_map/while/body/eval_jaxpr/reduce_sum | solution.py:75
  416.4 2.0 bitcast_dynamic-update-slice_fusion.4
  418.7 5.3 %fusion.252 = (f32[20,2,64]{2,1,0:T(2,128)S(1)}, f32[16,20,2,64]{3,2,1,0:T(2,128)}) fusion(f32[16,20,2,64]{3,0,2,1:T(8,128)S(1)} %bitcast.646, f32[16,20,2,64]{3,2,1,0:T(2,128)S(1)} %copy.124), kind=kLoop, calls=%fused_computation.8.clone.1 | loop fusion | flops 4544000 | bytes 501760 | tf_op jit(solution)/shard_map/while/body/eval_jaxpr/reduce_sum | solution.py:75
  424.5 2.0 bitcast_dynamic-update-slice_fusion.4
  426.7 5.3 %fusion.252 = (f32[20,2,64]{2,1,0:T(2,128)S(1)}, f32[16,20,2,64]{3,2,1,0:T(2,128)}) fusion(f32[16,20,2,64]{3,0,2,1:T(8,128)S(1)} %bitcast.646, f32[16,20,2,64]{3,2,1,0:T(2,128)S(1)} %copy.124), kind=kLoop, calls=%fused_computation.8.clone.1 | loop fusion | flops 4544000 | bytes 501760 | tf_op jit(solution)/shard_map/while/body/eval_jaxpr/reduce_sum | solution.py:75
  432.5 2.0 bitcast_dynamic-update-slice_fusion.4
  434.4 4.3 reshape.2183
  438.7 26.7 %all_to_all.54 = bf16[16,2,12800]{2,1,0:T(2,128)(2,1)S(1)} all-to-all(bf16[16,2,12800]{2,1,0:T(2,128)(2,1)S(1)} %reshape.2183), channel_id=1, replica_groups=mesh['ens'=16,'lat'=32] {'ens'}, dimensions={0} | all-to-all | bytes 1638400 | tf_op jit(solution)/shard_map/all_to_all | solution.py:105
  466.4 1.3 copy.93
  468.8 3.3 fusion.192
  472.3 1.7 copy.96
  474.0 2.0 reshape.2185
  476.0 9.5 %all-to-all-start.3 = ((bf16[32,2,7680]{2,1,0:T(2,128)(2,1)}), bf16[32,2,7680]{2,1,0:T(2,128)(2,1)S(1)}, u32[]{:S(2)}, u32[]{:S(2)}) async-start(bf16[32,2,7680]{2,1,0:T(2,128)(2,1)} %reshape.2185), calls=%async_computation.3 | async-start | bytes 1966080 | tf_op jit(solution)/shard_map/all_to_all | solution.py:114
  486.1 26.1 %all-to-all-done.3 = bf16[32,2,7680]{2,1,0:T(2,128)(2,1)S(1)} async-done(((bf16[32,2,7680]{2,1,0:T(2,128)(2,1)}), bf16[32,2,7680]{2,1,0:T(2,128)(2,1)S(1)}, u32[]{:S(2)}, u32[]{:S(2)}) %all-to-all-start.3) | async-done | bytes 983072 | tf_op jit(solution)/shard_map/all_to_all | solution.py:114
  512.2 1.2 reshape.2186
  513.5 1.4 copy.98
  514.8 2.3 fusion.195
  (566 shorter events, 66.0 us)
Async XLA Ops:
  6.3 0.8 copy-start
  6.3 1.0 copy-start.2
  14.0 286.8 %all-to-all-start = ((bf16[32,2,7680]{2,1,0:T(2,128)(2,1)}), bf16[32,2,7680]{2,1,0:T(2,128)(2,1)S(1)}, u32[]{:S(2)}, u32[]{:S(2)}) async-start(bf16[32,2,7680]{2,1,0:T(2,128)(2,1)} %reshape.2179), calls=%async_computation | async-start | bytes 1966080 | tf_op jit(solution)/shard_map/all_to_all | solution.py:98
  315.5 31.4 %all-to-all-start.1 = ((bf16[16,2,12800]{2,1,0:T(2,128)(2,1)}), bf16[16,2,12800]{2,1,0:T(2,128)(2,1)S(1)}, u32[]{:S(2)}, u32[]{:S(2)}) async-start(bf16[16,2,12800]{2,1,0:T(2,128)(2,1)} %reshape.2181), calls=%async_computation.1 | async-start | bytes 1638400 | tf_op jit(solution)/shard_map/all_to_all | solution.py:103
  476.0 36.2 %all-to-all-start.3 = ((bf16[32,2,7680]{2,1,0:T(2,128)(2,1)}), bf16[32,2,7680]{2,1,0:T(2,128)(2,1)S(1)}, u32[]{:S(2)}, u32[]{:S(2)}) async-start(bf16[32,2,7680]{2,1,0:T(2,128)(2,1)} %reshape.2185), calls=%async_computation.3 | async-start | bytes 1966080 | tf_op jit(solution)/shard_map/all_to_all | solution.py:114
  513.4 1.4 copy-start.1
  513.4 1.4 copy-start.3
where the time goes:
time: 521 us; the launch traced here: 517 us
  loops' own time  220 us (42%)
  other arithmetic  123 us (24%)
  local copies, waits for them, and re-layouts  55 us (11%)
  waiting for transfers between devices  49.4 us (9%)
  starting transfers between devices  31.3 us (6%)
  blocking collectives  26.7 us (5%)
  matrix products  11.5 us (2%)
    another operation x1, loops' own time, legendre_rows(): _, rows_out = lax.scan(block_step, initial, starts)  219 us
    reduce_sum x10, other arithmetic, crps_terms(): jnp.sum(pair_abs - SOFTNESS, axis=(0, 1))  53 us
    while x310, other arithmetic  32.5 us
    all_to_all x1, blocking collectives, body(): lax.all_to_all(coef_grad.astype(jnp.bfloat16), 'ens', split_axis=1, conca...  26.7 us
    all_to_all x1, waiting for transfers between devices, body(): lax.all_to_all(returned, 'lat', split_axis=1, concat_axis=0, tiled=True)  26.1 us
    all_to_all x1, waiting for transfers between devices, body(): lax.all_to_all(spectra[:, None], 'ens', split_axis=2, concat_axis=1, tile...  23.3 us
    dynamic_update_slice x10, other arithmetic, body(): coef_grad, totals = lax.map(crps_terms, received.astype(jnp.float32))  19.6 us
    unnamed x16, local copies, waits for them, and re-layouts  15.6 us
  transfers between devices with their start and end apart: 3, of which 2 were waited for; matrix products, arithmetic and copies ran while one was open for 11% of the time, Pallas kernels for 0%

commit v1 on v0

v1 whole, which is shorter than its diff:
```python
import math

import jax
import jax.numpy as jnp
import numpy as np
from jax import lax
from jax.experimental import pallas as pl
from jax.experimental.pallas import tpu as pltpu
from jax.sharding import PartitionSpec as P

SOFT2 = 0.1 * 0.1
CEILING = 2.0**60
SHRINK = 2.0 ** (-60)
LOG_SHIFT = 60.0 * math.log(2.0)
NLON, NLAT, DEG, MEM = 720, 384, 320, 16
GROUPS, VB = 5, 16
LANE = 128
MESH_AXES = ("ens", "lat")


def message_order():
    g, v, j = np.meshgrid(np.arange(GROUPS), np.arange(VB), np.arange(16), indexing="ij")
    extra = j - 8
    row = np.where(j < 8, j, 2 * extra + (g >= 3))
    lane = np.where(j < 8, 16 * g + v, 80 + 16 * (g - 3 * (g >= 3)) + v)
    place = np.where(j < 12, row * LANE + lane, -1).reshape(-1)
    return (place[:, None] == np.arange(8 * LANE)[None, :]).astype(jnp.bfloat16)


def latitude_order():
    row = np.arange(256)
    jb, c = row // 8, row % 8
    return np.concatenate([12 * jb + c, 12 * jb + 8 + c // 2])


def dot(a, b, dims=((1,), (0,))):
    return lax.dot_general(a, b, (dims, ((), ())), preferred_element_type=jnp.float32)


SIN_TERMS = [(-1) ** n / math.factorial(2 * n + 1) for n in range(7)]


def fourier_block(wave, part):
    lon = lax.broadcasted_iota(jnp.int32, (32, NLON), 1).astype(jnp.float32)
    turn = wave * lon + 180.0 * part
    turn = turn - NLON * jnp.floor((turn + 0.5) * (1.0 / NLON))
    x = (jnp.abs(turn - 360.0) - 180.0) * (math.pi / 360.0)
    x2 = x * x
    total = SIN_TERMS[6]
    for term in SIN_TERMS[5::-1]:
        total = total * x2 + term
    return total * x * (1.0 / math.sqrt(NLON))


def forward_kernel(wave_ref, order_ref, members_ref, analysis_ref, sent_ref, table_ref, dev, rows):
    @pl.when(pl.program_id(0) == 0)
    def _():
        dev[...] = jnp.zeros_like(dev)
        for g in range(GROUPS):
            for sb in range(4):
                pair = 5 * sb + g
                wave = wave_ref[:, pair // 2 : pair // 2 + 1]
                at = g * LANE + sb * 32
                table_ref[at : at + 32, :] = fourier_block(wave, pair % 2).astype(jnp.bfloat16)

    dev[:, 0:12, :] = members_ref[0].astype(jnp.float32) - analysis_ref[...].astype(jnp.float32)
    deviation = dev[...].reshape(256, NLON).astype(jnp.bfloat16)
    fourier = dot(table_ref[...], deviation, ((1,), (1,))).astype(jnp.bfloat16)
    wide = jnp.concatenate([fourier[g * LANE : (g + 1) * LANE] for g in range(GROUPS)], axis=1)
    placed = dot(wide, order_ref[...])
    for c in range(8):
        rows[pl.ds(c, LANE, stride=8), :] = placed[:, c * LANE : (c + 1) * LANE]
    sent_ref[...] = rows[...].reshape(LANE, 8, LANE).astype(jnp.bfloat16)


def legendre_kernel(wave_ref, base_ref, cos_ref, logsin_ref, weight_ref, leg_ref, legt_ref, rows):
    wave = jnp.broadcast_to(wave_ref[...], (8, 512))
    wave2 = wave * wave
    cosine = jnp.broadcast_to(cos_ref[...], (8, 512))
    weight = jnp.broadcast_to(weight_ref[...], (8, 512))
    start_log = base_ref[...] + wave * logsin_ref[...]
    zero = jnp.zeros((8, 512), jnp.float32)

    def block(b, carry):
        for offset in range(8):
            previous, older, inverse, log_scale = carry
            index = b * 8 + offset
            degree = index.astype(jnp.float32)
            square = jnp.full((8, 512), degree * degree, jnp.float32)
            ratio = jnp.maximum(square - wave2, 1.0) / jnp.maximum(4.0 * square - 1.0, 1.0)
            factor = lax.rsqrt(ratio)
            current = factor * (cosine * previous - older * inverse)
            current = jnp.where(wave == degree, 1.0, current)
            too_large = jnp.abs(current) > CEILING
            shrink = jnp.where(too_large, SHRINK, 1.0)
            log_scale = jnp.where(too_large, log_scale + LOG_SHIFT, log_scale)
            current = current * shrink
            previous = previous * shrink
            value = weight * (current * jnp.exp(log_scale))
            for q in range(4):
                rows[q, pl.ds(pl.multiple_of(index * 8, 8), 8), :] = value[:, q * LANE : (q + 1) * LANE]
            carry = (current, previous, ratio * factor, log_scale)
        return carry

    lax.fori_loop(0, DEG // 8, block, (zero, zero, zero + 1.0, start_log))
    for s in range(3):
        for q in range(4):
            part = rows[q, pl.ds(s, DEG, stride=8), :]
            at = s * 512 + q * LANE
            leg_ref[:, at : at + LANE] = part.astype(jnp.bfloat16)
            padded = jnp.concatenate([part, jnp.zeros((64, LANE), jnp.float32)], axis=0)
            legt_ref[q * LANE : (q + 1) * LANE, s * DEG : (s + 1) * DEG] = padded.T[:, :DEG].astype(
                jnp.bfloat16
            )


def score_kernel(got_ref, leg_ref, legt_ref, sent_ref, coef, per):
    own_lat = lax.axis_index("lat")
    odd_block = lax.rem(lax.axis_index("ens"), 2)
    lane = lax.broadcasted_iota(jnp.int32, (256, LANE), 1)
    even_row = lax.rem(lax.broadcasted_iota(jnp.int32, (256, LANE), 0), 2) == 0
    slot_of = jnp.where(lane < 80, (lane // 16 + odd_block) // 2, -1)
    extra_slot = jnp.where(even_row == (lane < 48), slot_of, -1)

    def spectra_pair(pair, _):
        halves = []
        for k in range(2):
            first = pl.multiple_of((2 * pair + k) * 32, 32)
            main = got_ref[pl.ds(first, 32)].astype(jnp.float32).reshape(256, LANE)
            extra = jnp.where(even_row, pltpu.roll(main, 48, 1), pltpu.roll(main, 96, 1))
            stack = []
            for s in range(3):
                stack.append(jnp.where(slot_of == s, main, 0.0).astype(jnp.bfloat16))
                stack.append(jnp.where(extra_slot == s, extra, 0.0).astype(jnp.bfloat16))
            halves.append(jnp.concatenate(stack, axis=0))
        spectra = dot(leg_ref[...], jnp.concatenate(halves, axis=1))
        spectra = spectra.astype(jnp.bfloat16).astype(jnp.float32)
        for k in range(2):
            coef[2 * pair + k] = spectra[:, k * LANE : (k + 1) * LANE]
        return 0

    lax.fori_loop(0, MEM // 2, spectra_pair, 0)

    def degrees(tile, _):
        at = pl.ds(pl.multiple_of(tile * 8, 8), 8)
        z = [coef[e, at, :] for e in range(MEM)]
        pull = [None] * MEM
        inverse_sum = None
        for a in range(MEM):
            for b in range(a + 1, MEM):
                diff = z[a] - z[b]
                inverse = lax.rsqrt(diff * diff + SOFT2)
                term = diff * inverse
                inverse_sum = inverse if inverse_sum is None else inverse_sum + inverse
                pull[a] = term if pull[a] is None else pull[a] + term
                pull[b] = -term if pull[b] is None else pull[b] - term
        pair_abs = SOFT2 * inverse_sum
        single = None
        for e in range(MEM):
            square = z[e] * z[e] + SOFT2
            inverse = lax.rsqrt(square)
            soft = square * inverse
            single = soft if single is None else single + soft
            pair_abs = pair_abs + z[e] * pull[e]
            coef[e, at, :] = z[e] * inverse - pull[e] * (1.0 / (MEM - 1))
        per[at, :] = (single - 0.1 * MEM) * (1.0 / MEM) - (pair_abs - 0.1 * (MEM * (MEM - 1) // 2)) * (
            1.0 / (MEM * (MEM - 1))
        )
        return 0

    lax.fori_loop(0, DEG // 8, degrees, 0)

    row = lax.broadcasted_iota(jnp.int32, (LANE, LANE), 0)
    col = lax.broadcasted_iota(jnp.int32, (LANE, LANE), 1) - 112
    row_slot = jnp.where(row < 80, (row // 16 + odd_block) // 2, -1)
    col_slot = jnp.where((col >= 0) & (col < 15), (col + 25) // 5 - 5, -2)
    gather = jnp.where(row_slot == col_slot, 1.0, 0.0)
    summed = lax.dot_general(
        per[...],
        gather,
        (((1,), (0,)), ((), ())),
        precision=lax.Precision.HIGHEST,
        preferred_element_type=jnp.float32,
    )
    degree = lax.broadcasted_iota(jnp.int32, (DEG, LANE), 0)
    column = lax.broadcasted_iota(jnp.int32, (DEG, LANE), 1) - 110
    keep = (column >= 2) & (lax.rem(degree, 5) == lax.rem(column + 3, 5))
    summed = jnp.where(keep, summed, 0.0).astype(jnp.bfloat16)
    out_row = lax.broadcasted_iota(jnp.int32, (LANE, DEG), 0)
    out_deg = lax.broadcasted_iota(jnp.int32, (LANE, DEG), 1)
    want = (out_row // 8) * 4 + lax.rem(out_row, 8) // 2
    pick = (lax.rem(out_row, 2) == 1) & (out_deg // 5 == want)
    scores = dot(jnp.where(pick, 1.0, 0.0).astype(jnp.bfloat16), summed)
    per[0:LANE, :] = scores

    def returned_pair(pair, _):
        halves = []
        for k in range(2):
            grad = coef[2 * pair + k]
            halves.append(
                jnp.concatenate(
                    [jnp.where(slot_of[0:1] == s, grad, 0.0).astype(jnp.bfloat16) for s in range(3)], axis=0
                )
            )
        back = dot(legt_ref[...], jnp.concatenate(halves, axis=1))
        for k in range(2):
            main = back[0:256, k * LANE : (k + 1) * LANE]
            extra = back[256:512, k * LANE : (k + 1) * LANE]
            extra = jnp.where(even_row, pltpu.roll(extra, 80, 1), pltpu.roll(extra, 32, 1))
            message = jnp.where(lane < 80, main, extra).reshape(32, 8, LANE)
            member = 2 * pair + k
            own = lax.broadcasted_iota(jnp.int32, (32, 8, LANE), 0) == own_lat
            score = per[pl.ds(pl.multiple_of(member * 8, 8), 8), :][None]
            message = jnp.where(own, message + score, message)
            sent_ref[pl.ds(pl.multiple_of(member * 32, 32), 32)] = message.astype(jnp.bfloat16)
        return 0

    lax.fori_loop(0, MEM // 2, returned_pair, 0)


def inverse_kernel(got_ref, order_ref, table_ref, grid_ref, score_ref, rows):
    own_lat = lax.axis_index("lat")
    step = pl.program_id(0)
    rows[...] = got_ref[...].astype(jnp.float32).reshape(256 * 8, LANE)
    got = jnp.concatenate([rows[pl.ds(c, 256, stride=8), :] for c in range(8)], axis=1).astype(jnp.bfloat16)
    turned = dot(order_ref[...], got, ((1,), (1,))).astype(jnp.bfloat16)
    for half in range(2):
        left = jnp.concatenate(
            [turned[g * 256 : (g + 1) * 256, half * LANE : (half + 1) * LANE] for g in range(GROUPS)], axis=1
        )
        grid = dot(left, table_ref[...]).reshape(16, 16, NLON)[:, 0:12, :]
        grid_ref[0, half * 16 : (half + 1) * 16] = grid.astype(jnp.bfloat16)
    for sb in range(4):
        part = None
        for half in range(2):
            at = pl.multiple_of((half * LANE + sb * 32 + own_lat) * 8, 8)
            tile = rows[pl.ds(at, 8), :]
            part = tile if part is None else part + tile
        score_ref[sb] = jnp.where(step == 0, part, score_ref[sb] + part)


def body(members, analysis, wave_order):
    order = jnp.asarray(message_order())
    block_mib = 1 << 20
    waves = wave_order.astype(jnp.float32)
    sent, table = pl.pallas_call(
        forward_kernel,
        grid=(4,),
        in_specs=[
            pl.BlockSpec((32, 10), lambda i: (0, 0)),
            pl.BlockSpec((1280, 1024), lambda i: (0, 0)),
            pl.BlockSpec((1, 16, 12, NLON), lambda i: (0, i, 0, 0)),
            pl.BlockSpec((16, 12, NLON), lambda i: (i, 0, 0)),
        ],
        out_specs=[
            pl.BlockSpec((LANE, 8, LANE), lambda i: (i, 0, 0)),
            pl.BlockSpec((640, NLON), lambda i: (0, 0)),
        ],
        out_shape=[
            jax.ShapeDtypeStruct((512, 8, LANE), jnp.bfloat16),
            jax.ShapeDtypeStruct((640, NLON), jnp.bfloat16),
        ],
        scratch_shapes=[pltpu.VMEM((16, 16, NLON), jnp.float32), pltpu.VMEM((1024, LANE), jnp.float32)],
        compiler_params=pltpu.CompilerParams(vmem_limit_bytes=32 * block_mib),
        cost_estimate=pl.CostEstimate(flops=3 * 10**9, bytes_accessed=8 * 10**6, transcendentals=0),
        name="forward",
    )(waves.reshape(32, 10), order, members, analysis)
    got = lax.all_to_all(sent, MESH_AXES, 0, 0, tiled=True)

    own = lax.axis_index("lat") * 10 + (5 * lax.rem(lax.axis_index("ens"), 4)) // 2
    slots = lax.dynamic_slice_in_dim(waves, own, 3)
    slots = jnp.concatenate([slots, jnp.broadcast_to(slots[2:3], (5,))]).reshape(8, 1)
    base = 0.5 * (
        lax.lgamma(slots + 1.5) - lax.lgamma(slots + 1.0) - lax.lgamma(jnp.float32(1.5)) + math.log(0.5)
    )
    colatitude = (latitude_order() + 0.5) * (math.pi / NLAT)
    constants = [np.cos(colatitude), np.log(np.sin(colatitude)), math.sqrt(math.pi / NLAT) * np.sin(colatitude)]
    constants = [jnp.asarray(c[None].astype(np.float32)) for c in constants]
    legendre, legendre_t = pl.pallas_call(
        legendre_kernel,
        out_shape=[
            jax.ShapeDtypeStruct((DEG, 1536), jnp.bfloat16),
            jax.ShapeDtypeStruct((512, 960), jnp.bfloat16),
        ],
        scratch_shapes=[pltpu.VMEM((4, DEG * 8, LANE), jnp.float32)],
        compiler_params=pltpu.CompilerParams(vmem_limit_bytes=32 * block_mib),
        cost_estimate=pl.CostEstimate(flops=10**8, bytes_accessed=2 * 10**6, transcendentals=3 * 10**6),
        name="legendre",
    )(slots, base, *constants)

    sent = pl.pallas_call(
        score_kernel,
        out_shape=jax.ShapeDtypeStruct((512, 8, LANE), jnp.bfloat16),
        scratch_shapes=[pltpu.VMEM((MEM, DEG, LANE), jnp.float32), pltpu.VMEM((DEG, LANE), jnp.float32)],
        compiler_params=pltpu.CompilerParams(vmem_limit_bytes=40 * block_mib),
        cost_estimate=pl.CostEstimate(flops=6 * 10**9, bytes_accessed=5 * 10**6, transcendentals=5 * 10**6),
        name="score",
    )(got, legendre, legendre_t)
    got = lax.all_to_all(sent, MESH_AXES, 0, 0, tiled=True)

    grid_grad, parts = pl.pallas_call(
        inverse_kernel,
        grid=(2,),
        in_specs=[
            pl.BlockSpec((256, 8, LANE), lambda i: (i, 0, 0)),
            pl.BlockSpec((1280, 1024), lambda i: (0, 0)),
            pl.BlockSpec((640, NLON), lambda i: (0, 0)),
        ],
        out_specs=[
            pl.BlockSpec((1, 32, 12, NLON), lambda i: (0, i, 0, 0)),
            pl.BlockSpec((4, 8, LANE), lambda i: (0, 0, 0)),
        ],
        out_shape=[
            jax.ShapeDtypeStruct((1, 64, 12, NLON), jnp.bfloat16),
            jax.ShapeDtypeStruct((4, 8, LANE), jnp.float32),
        ],
        scratch_shapes=[pltpu.VMEM((2048, LANE), jnp.float32)],
        compiler_params=pltpu.CompilerParams(vmem_limit_bytes=40 * block_mib),
        cost_estimate=pl.CostEstimate(flops=3 * 10**9, bytes_accessed=8 * 10**6, transcendentals=0),
        name="inverse",
    )(got, order, table)
    parts = parts[:, 1::2, 112:127].reshape(4, 4, 3, 5).transpose(0, 2, 1, 3).reshape(4, 3, 20) / (2 * 64)
    halves = [
        jnp.concatenate([parts[k, :2], parts[k, 2:] + parts[k + 1, :1], parts[k + 1, 1:]]) for k in (0, 2)
    ]
    return (grid_grad, jnp.concatenate(halves))


def solution(mesh):
    placed = (P("ens", None, "lat", None), P(None, "lat", None), P())
    return jax.shard_map(
        body,
        mesh=mesh,
        in_specs=placed,
        out_specs=(P("ens", None, "lat", None), P("lat", "ens")),
        check_vma=False,
    )
```

time: 521 us -> 137 us (0.26)
  loops' own time: 220 us -> 0 us
  other arithmetic: 123 us -> 1.51 us
  local copies, waits for them, and re-layouts: 55 us -> 9.66 us
  Pallas kernels: 0 us -> 34.3 us
  waiting for transfers between devices: 49.4 us -> 25.5 us
  blocking collectives: 26.7 us -> 42.9 us
  matrix products: 11.5 us -> 0 us
  starting transfers between devices: 31.3 us -> 22.2 us
    another operation x2 -> x0, loops' own time: 220 us -> none  [the longest x1 219 us: legendre_rows(): _, rows_out = lax.scan(block_step, initial, starts)]
    reduce_sum x30 -> x0, other arithmetic: 57.4 us -> none  [the longest x10 53 us: crps_terms(): jnp.sum(pair_abs - SOFTNESS, axis=(0, 1))]
    pallas_call x0 -> x4, Pallas kernels: none -> 34.3 us  [the longest x1 16.1 us: body(): pl.pallas_call(score_kernel, out_shape=jax.ShapeDtypeStruct((512, 8, LANE...]
    while x310 -> x0, other arithmetic: 32.5 us -> none
    all_to_all x3 -> x1, waiting for transfers between devices: 49.4 us -> 25.5 us  [body(): got = lax.all_to_all(sent, MESH_AXES, 0, 0, tiled=True)]
    dynamic_update_slice x10 -> x0, other arithmetic: 19.6 us -> none  [body(): coef_grad, totals = lax.map(crps_terms, received.astype(jnp.float32))]
    all_to_all x1, blocking collectives: 26.7 us -> 42.9 us  [body(): got = lax.all_to_all(sent, MESH_AXES, 0, 0, tiled=True)]
    all_to_all x5 -> x0, local copies, waits for them, and re-layouts: 12.3 us -> none  [the longest x2 6.7 us: body(): lax.all_to_all(fourier, 'lat', split_axis=0, concat_axis=1, tiled=True)]
  transfers between devices with their start and end apart: 3 -> 1, of which waited for: 2 -> 1; matrix products, arithmetic and copies ran while one was open for 11% -> 1% of each run, Pallas kernels for 0% -> 3%
where the time goes in v1:
time: 137 us
  blocking collectives  42.9 us (31%)
  Pallas kernels  34.3 us (25%)
  waiting for transfers between devices  25.5 us (19%)
  starting transfers between devices  22.2 us (16%)
  local copies, waits for them, and re-layouts  9.66 us (7%)
  other arithmetic  1.51 us (1%)
    all_to_all x1, blocking collectives, body(): got = lax.all_to_all(sent, MESH_AXES, 0, 0, tiled=True)  42.9 us
    all_to_all x1, waiting for transfers between devices, body(): got = lax.all_to_all(sent, MESH_AXES, 0, 0, tiled=True)  25.5 us
    all_to_all x1, starting transfers between devices, body(): got = lax.all_to_all(sent, MESH_AXES, 0, 0, tiled=True)  22.2 us
    pallas_call x1, Pallas kernels, body(): pl.pallas_call(score_kernel, out_shape=jax.ShapeDtypeStruct((512, 8, LANE...  16.1 us
    pallas_call x1, Pallas kernels, body(): pl.pallas_call(forward_kernel, grid=(4,), in_specs=[pl.BlockSpec((32, 10)...  8.15 us
    unnamed x19, local copies, waits for them, and re-layouts  7.24 us
    pallas_call x1, Pallas kernels, body(): pl.pallas_call(inverse_kernel, grid=(2,), in_specs=[pl.BlockSpec((256, 8,...  5.32 us
    pallas_call x1, Pallas kernels, body(): pl.pallas_call(legendre_kernel, out_shape=[jax.ShapeDtypeStruct((DEG, 153...  4.78 us
  transfers between devices with their start and end apart: 1, of which 1 were waited for; matrix products, arithmetic and copies ran while one was open for 1% of the time, Pallas kernels for 3%

profile of v1, /device:TPU:1, one launch (start us, length us, event | category | flops | bytes accessed | tf_op | source)
XLA Modules:
  0.0 136.8 jit_solution(6234968867152174577)
XLA Ops:
  0.6 0.0 copy-start.7
  0.6 0.8 convert_element_type.3
  1.4 0.1 reshape.176.wave_ref
  1.5 1.9 %copy.15.members_ref = bf16[1,64,12,720]{3,2,1,0:T(8,128)(2,1)S(1)} copy(bf16[1,64,12,720]{3,1,2,0:T(8,128)(2,1)} %param.7) | data formatting | bytes 2211840 | tf_op args[0]
  3.5 0.0 copy-done.7
  3.5 0.0 copy-start
  3.5 0.7 copy.16.analysis_ref
  4.2 1.1 copy-done
  5.2 8.2 %forward.1 = (bf16[512,8,128]{2,1,0:T(8,128)(2,1)}, bf16[640,720]{1,0:T(8,128)(2,1)S(1)}) custom-call(f32[32,10]{1,0:T(8,128)S(1)} %reshape.176.wave_ref, bf16[1280,1024]{1,0:T(8,128)(2,1)S(1)} %copy-done, bf16[1,64,12,720]{3,2,1,0:T(8,128)(2,1)S(1)} %copy.15.members_ref, bf16[64,12,720]{2,1,0:T(8,128)(2,1)S(1)} %copy.16.analysis_ref), custom_call_target="tpu_custom_call" | custom-call | flops 3000000000 | bytes 8000000 | tf_op jit(solution)/shard_map/forward/pallas_call | solution.py:246
  13.4 0.0 copy-start.2
  13.4 0.0 copy-start.3
  13.4 0.0 copy-start.4
  13.4 22.2 %all-to-all-start = ((bf16[512,8,128]{2,1,0:T(8,128)(2,1)}), bf16[512,8,128]{2,1,0:T(8,128)(2,1)S(1)}, u32[]{:S(2)}, u32[]{:S(2)}) async-start(bf16[512,8,128]{2,1,0:T(8,128)(2,1)} %get-tuple-element.8), calls=%async_computation | async-start | bytes 2097152 | tf_op jit(solution)/shard_map/all_to_all | solution.py:268
  35.6 0.1 dynamic_slice.3
  35.7 0.6 slice.30
  36.2 0.7 multiply_bitcast_fusion
  37.0 0.1 copy.17.wave_ref
  37.0 0.1 copy.18.base_ref
  37.1 0.0 copy-done.2
  37.1 0.0 copy-done.3
  37.1 0.0 copy-done.4
  37.1 4.8 %legendre.1 = (bf16[320,1536]{1,0:T(8,128)(2,1)S(1)}, bf16[512,960]{1,0:T(8,128)(2,1)S(1)}) custom-call(f32[8,1]{1,0:T(8,128)S(1)} %copy.17.wave_ref, f32[8,1]{1,0:T(8,128)S(1)} %copy.18.base_ref, f32[1,512]{1,0:T(1,128)S(1)} %copy-done.2, f32[1,512]{1,0:T(1,128)S(1)} %copy-done.3, f32[1,512]{1,0:T(1,128)S(1)} %copy-done.4), custom_call_target="tpu_custom_call" | custom-call | flops 100000000 | bytes 2000000 | tf_op jit(solution)/shard_map/legendre/pallas_call | solution.py:279
  41.9 0.0 copy-start.5
  41.9 1.0 copy-done.5
  42.9 25.5 %all-to-all-done.got_ref = bf16[512,8,128]{2,1,0:T(8,128)(2,1)S(1)} async-done(((bf16[512,8,128]{2,1,0:T(8,128)(2,1)}), bf16[512,8,128]{2,1,0:T(8,128)(2,1)S(1)}, u32[]{:S(2)}, u32[]{:S(2)}) %all-to-all-start) | async-done | bytes 1048608 | tf_op jit(solution)/shard_map/all_to_all | solution.py:268
  68.4 0.0 copy-start.6
  68.4 1.2 copy-done.6
  69.6 0.0 copy-start.1
  69.6 16.1 %score.1 = bf16[512,8,128]{2,1,0:T(8,128)(2,1)S(1)} custom-call(bf16[512,8,128]{2,1,0:T(8,128)(2,1)S(1)} %all-to-all-done.got_ref, bf16[320,1536]{1,0:T(8,128)(2,1)S(1)} %get-tuple-element.9.leg_ref, bf16[512,960]{1,0:T(8,128)(2,1)S(1)} %copy-done.6), custom_call_target="tpu_custom_call" | custom-call | flops 6000000000 | bytes 5000000 | tf_op jit(solution)/shard_map/score/pallas_call | solution.py:291
  85.7 42.9 %all_to_all.10.got_ref = bf16[512,8,128]{2,1,0:T(8,128)(2,1)S(1)} all-to-all(bf16[512,8,128]{2,1,0:T(8,128)(2,1)S(1)} %score.1), channel_id=1, replica_groups=mesh['ens'=16,'lat'=32] {'ens','lat'}, dimensions={0} | all-to-all | bytes 2097152 | tf_op jit(solution)/shard_map/all_to_all | solution.py:299
  128.6 0.0 copy-done.1
  128.6 5.3 %inverse.1 = (bf16[1,64,12,720]{3,2,1,0:T(8,128)(2,1)S(1)}, f32[4,8,128]{2,1,0:T(8,128)S(1)}) custom-call(bf16[512,8,128]{2,1,0:T(8,128)(2,1)S(1)} %all_to_all.10.got_ref, bf16[1280,1024]{1,0:T(8,128)(2,1)S(1)} %copy-done.1, bf16[640,720]{1,0:T(8,128)(2,1)S(1)} %get-tuple-element.11.table_ref), custom_call_target="tpu_custom_call" | custom-call | flops 3000000000 | bytes 8000000 | tf_op jit(solution)/shard_map/inverse/pallas_call | solution.py:301
  133.9 0.1 slice.31
  134.0 0.1 div.25
  134.1 0.1 div.27
  134.2 1.4 copy.20
  135.6 1.2 concatenate.7
  (4 shorter events, 0.0 us)
Async XLA Ops:
  0.6 2.8 %copy-start.7 = (bf16[64,12,720]{2,0,1:T(8,128)(2,1)S(1)}, bf16[64,12,720]{2,0,1:T(8,128)(2,1)}, u32[]{:S(2)}) copy-start(bf16[64,12,720]{2,0,1:T(8,128)(2,1)} %param.8) | copy-start | bytes 3317764
  3.5 1.7 %copy-start = (bf16[1280,1024]{1,0:T(8,128)(2,1)S(1)}, bf16[1280,1024]{1,0:T(8,128)(2,1)}, u32[]{:S(2)}) copy-start(bf16[1280,1024]{1,0:T(8,128)(2,1)} %constant.117.clone.order_ref) | copy-start | bytes 7864324
  13.4 23.8 %copy-start.2 = (f32[1,512]{1,0:T(1,128)S(1)}, f32[1,512]{1,0:T(1,128)}, u32[]{:S(2)}) copy-start(f32[1,512]{1,0:T(1,128)} %constant.118.clone.cos_ref) | copy-start | bytes 6148
  13.4 23.8 %copy-start.3 = (f32[1,512]{1,0:T(1,128)S(1)}, f32[1,512]{1,0:T(1,128)}, u32[]{:S(2)}) copy-start(f32[1,512]{1,0:T(1,128)} %constant.119.clone.logsin_ref) | copy-start | bytes 6148
  13.4 23.8 %copy-start.4 = (f32[1,512]{1,0:T(1,128)S(1)}, f32[1,512]{1,0:T(1,128)}, u32[]{:S(2)}) copy-start(f32[1,512]{1,0:T(1,128)} %constant.120.clone.weight_ref) | copy-start | bytes 6148
  13.4 55.0 %all-to-all-start = ((bf16[512,8,128]{2,1,0:T(8,128)(2,1)}), bf16[512,8,128]{2,1,0:T(8,128)(2,1)S(1)}, u32[]{:S(2)}, u32[]{:S(2)}) async-start(bf16[512,8,128]{2,1,0:T(8,128)(2,1)} %get-tuple-element.8), calls=%async_computation | async-start | bytes 2097152 | tf_op jit(solution)/shard_map/all_to_all | solution.py:268
  41.9 1.0 copy-start.5
  68.4 1.2 copy-start.6
  69.6 59.0 %copy-start.1 = (bf16[1280,1024]{1,0:T(8,128)(2,1)S(1)}, bf16[1280,1024]{1,0:T(8,128)(2,1)}, u32[]{:S(2)}) copy-start(bf16[1280,1024]{1,0:T(8,128)(2,1)} %constant.117.clone.order_ref) | copy-start | bytes 7864324

commit v2 on v1

v2 whole, which is shorter than its diff:
```python
import math

import jax
import jax.numpy as jnp
import numpy as np
from jax import lax
from jax.experimental import pallas as pl
from jax.experimental.pallas import tpu as pltpu
from jax.sharding import PartitionSpec as P

SOFT2 = 0.1 * 0.1
CEILING = 2.0**60
SHRINK = 2.0 ** (-60)
LOG_SHIFT = 60.0 * math.log(2.0)
NLON, NLAT, DEG, MEM = 720, 384, 320, 16
GROUPS, VB = 5, 16
LANE = 128
MESH_AXES = ("ens", "lat")


def message_order(rows, width):
    shape = (GROUPS * rows, width)
    row = lax.broadcasted_iota(jnp.int32, shape, 0)
    lane = lax.broadcasted_iota(jnp.int32, shape, 1)
    g, inner = row // rows, row % rows
    k, v = inner % 64 // VB, row % VB
    second = jnp.where(g >= 3, 1, 0)
    plain = k * LANE + 16 * g + v
    extra = second * LANE + 80 + 16 * (g - 3 * second) + v
    place = jnp.where(k < 2, plain, jnp.where(k == 2, extra, -1024))
    place = place + 256 * (inner // 64)
    return jnp.where(place == lane, 1.0, 0.0).astype(jnp.bfloat16)


def latitude_order():
    row = np.arange(256)
    jb, c = row // 8, row % 8
    return np.concatenate([12 * jb + c, 12 * jb + 8 + c // 2])


def dot(a, b, dims=((1,), (0,))):
    return lax.dot_general(a, b, (dims, ((), ())), preferred_element_type=jnp.float32)


SIN_TERMS = [(-1) ** n / math.factorial(2 * n + 1) for n in range(7)]


def fourier_block(wave, part):
    lon = lax.broadcasted_iota(jnp.int32, (32, NLON), 1).astype(jnp.float32)
    turn = wave * lon + 180.0 * part
    turn = turn - NLON * jnp.floor((turn + 0.5) * (1.0 / NLON))
    x = (jnp.abs(turn - 360.0) - 180.0) * (math.pi / 360.0)
    x2 = x * x
    total = SIN_TERMS[6]
    for term in SIN_TERMS[5::-1]:
        total = total * x2 + term
    return total * x * (1.0 / math.sqrt(NLON))


def forward_kernel(wave_ref, members_hbm, analysis_hbm, sent_ref, table_ref, members, analysis, rows, sems):
    loads = [
        pltpu.make_async_copy(members_hbm, members, sems.at[0]),
        pltpu.make_async_copy(analysis_hbm, analysis, sems.at[1]),
    ]
    for load in loads:
        load.start()
    waves = jnp.broadcast_to(wave_ref[...].reshape(1, DEG).astype(jnp.float32), (32, DEG))
    ahead = lax.broadcasted_iota(jnp.int32, (32, DEG), 1) - 10 * lax.broadcasted_iota(jnp.int32, (32, DEG), 0)
    columns = [jnp.sum(jnp.where(ahead == k, waves, 0.0), axis=1, keepdims=True) for k in range(10)]
    for g in range(GROUPS):
        for sb in range(4):
            pair = 5 * sb + g
            at = g * LANE + sb * 32
            table_ref[at : at + 32, :] = fourier_block(columns[pair // 2], pair % 2).astype(jnp.bfloat16)
    order = message_order(LANE, 512)
    for load in loads:
        load.wait()

    deviation = (members[0].astype(jnp.float32) - analysis[...].astype(jnp.float32)).astype(jnp.bfloat16)
    blank = jnp.zeros((VB, NLON), jnp.bfloat16)
    for h in range(2):
        pieces = []
        for t in range(4):
            for vb in (2 * h, 2 * h + 1):
                pieces += [deviation[j, vb * VB : (vb + 1) * VB] for j in (2 * t, 2 * t + 1, 8 + t)] + [blank]
        fourier = dot(table_ref[...], jnp.concatenate(pieces, axis=0), ((1,), (1,))).astype(jnp.bfloat16)
        wide = jnp.concatenate(
            [
                jnp.concatenate(
                    [fourier[g * LANE : (g + 1) * LANE, t * LANE : (t + 1) * LANE] for g in range(GROUPS)],
                    axis=1,
                )
                for t in range(4)
            ],
            axis=0,
        )
        placed = dot(wide, order)
        for t in range(4):
            for q in range(4):
                at = (q // 2) * LANE * 8 + 2 * t + q % 2
                rows[pl.ds(at, LANE, stride=8), :] = placed[
                    t * LANE : (t + 1) * LANE, q * LANE : (q + 1) * LANE
                ]
        sent_ref[h * 256 : (h + 1) * 256] = rows[...].reshape(256, 8, LANE).astype(jnp.bfloat16)


def legendre_kernel(wave_ref, base_ref, cos_ref, logsin_ref, weight_ref, leg_ref, rows):
    wave = jnp.broadcast_to(wave_ref[...], (8, 512))
    wave2 = wave * wave
    cosine = jnp.broadcast_to(cos_ref[...], (8, 512))
    weight = jnp.broadcast_to(weight_ref[...], (8, 512))
    start_log = base_ref[...] + wave * logsin_ref[...]
    zero = jnp.zeros((8, 512), jnp.float32)

    def block(b, carry):
        for offset in range(8):
            previous, older, inverse, log_scale = carry
            index = b * 8 + offset
            degree = index.astype(jnp.float32)
            square = jnp.full((8, 512), degree * degree, jnp.float32)
            ratio = jnp.maximum(square - wave2, 1.0) / jnp.maximum(4.0 * square - 1.0, 1.0)
            factor = lax.rsqrt(ratio)
            current = factor * (cosine * previous - older * inverse)
            current = jnp.where(wave == degree, 1.0, current)
            too_large = jnp.abs(current) > CEILING
            shrink = jnp.where(too_large, SHRINK, 1.0)
            log_scale = jnp.where(too_large, log_scale + LOG_SHIFT, log_scale)
            current = current * shrink
            previous = previous * shrink
            value = weight * (current * jnp.exp(log_scale))
            for q in range(4):
                rows[q, pl.ds(pl.multiple_of(index * 8, 8), 8), :] = value[:, q * LANE : (q + 1) * LANE]
            carry = (current, previous, ratio * factor, log_scale)
        return carry

    lax.fori_loop(0, DEG // 8, block, (zero, zero, zero + 1.0, start_log))
    for s in range(3):
        for q in range(4):
            part = rows[q, pl.ds(s, DEG, stride=8), :]
            at = s * 512 + q * LANE
            leg_ref[:, at : at + LANE] = part.astype(jnp.bfloat16)


def pair_terms(z):
    pull = [None] * MEM
    inverse_sum = None
    for a in range(MEM):
        for b in range(a + 1, MEM):
            diff = z[a] - z[b]
            inverse = lax.rsqrt(diff * diff + SOFT2)
            term = diff * inverse
            inverse_sum = inverse if inverse_sum is None else inverse_sum + inverse
            pull[a] = term if pull[a] is None else pull[a] + term
            pull[b] = -term if pull[b] is None else pull[b] - term
    pair_abs = SOFT2 * inverse_sum
    single = None
    grads = []
    for e in range(MEM):
        square = z[e] * z[e] + SOFT2
        inverse = lax.rsqrt(square)
        soft = square * inverse
        single = soft if single is None else single + soft
        pair_abs = pair_abs + z[e] * pull[e]
        grads.append(z[e] * inverse - pull[e] * (1.0 / (MEM - 1)))
    pairs = MEM * (MEM - 1)
    return grads, (single - 0.1 * MEM) * (1.0 / MEM) - (pair_abs - 0.1 * (pairs // 2)) * (1.0 / pairs)


def score_kernel(got_ref, leg_ref, sent_ref, turned, coef, sums, scores):
    own_lat = lax.axis_index("lat")
    odd_block = lax.rem(lax.axis_index("ens"), 2)
    even = lax.rem(lax.broadcasted_iota(jnp.int32, (48, 256), 1), 2) == 0
    unit = lax.broadcasted_iota(jnp.int32, (256, 256), 0) == lax.broadcasted_iota(jnp.int32, (256, 256), 1)
    unit = jnp.where(unit, 1.0, 0.0).astype(jnp.bfloat16)

    def slot_lanes(g):
        return pl.ds(pl.multiple_of((g + odd_block) // 2 * 512, 512), 512)

    def turn(member, _):
        message = got_ref[pl.ds(pl.multiple_of(member * 32, 32), 32)].astype(jnp.float32)
        message = message.reshape(256, LANE).astype(jnp.bfloat16)
        rows = dot(unit[:LANE, :LANE], message, ((1,), (1,)))
        at = pl.ds(pl.multiple_of(member * VB, VB), VB)
        low = jnp.where(even, rows[80:128], 0.0).astype(jnp.bfloat16)
        high = jnp.where(even, 0.0, rows[80:128]).astype(jnp.bfloat16)
        for g in range(GROUPS):
            turned[g, at, 0:256] = rows[g * VB : (g + 1) * VB].astype(jnp.bfloat16)
            extra = low[g * VB : (g + 1) * VB] if g < 3 else high[(g - 3) * VB : (g - 2) * VB]
            turned[g, at, 256:512] = extra
        return 0

    lax.fori_loop(0, MEM, turn, 0, unroll=4)

    first_half = lax.broadcasted_iota(jnp.int32, (8, LANE), 1) < 64

    def group(g, _):
        spectra = dot(turned[g], leg_ref[:, slot_lanes(g)], ((1,), (1,)))
        coef[:, 0:DEG] = spectra.astype(jnp.bfloat16).astype(jnp.float32)
        for q in range(2):
            lanes = slice(q * LANE, (q + 1) * LANE)
            total = None
            for r in range(2):
                grads, per = pair_terms([coef[e * VB + r * 8 : e * VB + r * 8 + 8, lanes] for e in range(MEM)])
                for e in range(MEM):
                    coef[e * VB + r * 8 : e * VB + r * 8 + 8, lanes] = grads[e]
                total = per if total is None else total + per
            sums[g, :, lanes] = total
        lanes = slice(2 * LANE, 3 * LANE)
        packed = []
        for e in range(MEM):
            top, bottom = coef[e * VB : e * VB + 8, lanes], coef[e * VB + 8 : e * VB + VB, lanes]
            packed.append(jnp.where(first_half, top, pltpu.roll(bottom, 64, 1)))
        grads, per = pair_terms(packed)
        for e in range(MEM):
            coef[e * VB : e * VB + 8, lanes] = grads[e]
            coef[e * VB + 8 : e * VB + VB, lanes] = pltpu.roll(grads[e], 64, 1)
        sums[g, :, lanes] = per + pltpu.roll(per, 64, 1)
        grad = coef[:, 0:DEG].astype(jnp.bfloat16)
        turned[g] = dot(grad, leg_ref[:, slot_lanes(g)]).astype(jnp.bfloat16)
        return 0

    lax.fori_loop(0, GROUPS, group, 0)

    place = lax.broadcasted_iota(jnp.int32, (16, DEG), 0)
    same = lax.rem(lax.broadcasted_iota(jnp.int32, (16, DEG), 1), 5) == lax.rem(place, 5)
    spread = jnp.zeros((16, DEG), jnp.float32)
    for g in range(GROUPS):
        mine = same & (place < 15) & (place // 5 == (g + odd_block) // 2)
        score = jnp.sum(sums[g], axis=0, keepdims=True)[:, 0:DEG]
        spread = spread + jnp.where(mine, jnp.broadcast_to(score, (16, DEG)), 0.0)
    spread = jnp.concatenate([jnp.zeros((112, DEG), jnp.float32), spread], axis=0).astype(jnp.bfloat16)
    out_row = lax.broadcasted_iota(jnp.int32, (LANE, DEG), 0)
    out_deg = lax.broadcasted_iota(jnp.int32, (LANE, DEG), 1)
    pick = (lax.rem(out_row, 2) == 1) & (out_deg // 5 == (out_row // 8) * 4 + lax.rem(out_row, 8) // 2)
    scores[...] = dot(jnp.where(pick, 1.0, 0.0).astype(jnp.bfloat16), spread, ((1,), (1,)))

    def send(pair, _):
        rows = []
        for k in range(2):
            at = pl.ds(pl.multiple_of((2 * pair + k) * VB, VB), VB)
            rows += [turned[g, at, 0:256] for g in range(GROUPS)]
            extra = [turned[g, at, 256:512].astype(jnp.float32) for g in range(GROUPS)]
            blank = jnp.zeros((VB, 256), jnp.float32)
            extra = jnp.where(even, jnp.concatenate(extra[:3]), jnp.concatenate(extra[3:] + [blank]))
            rows.append(extra.astype(jnp.bfloat16))
        back = dot(unit, jnp.concatenate(rows, axis=0), ((1,), (1,)))
        for k in range(2):
            member = 2 * pair + k
            message = back[:, k * LANE : (k + 1) * LANE].reshape(32, 8, LANE)
            sent_ref[pl.ds(pl.multiple_of(member * 32, 32), 32)] = message.astype(jnp.bfloat16)
            score = scores[pl.ds(pl.multiple_of(member * 8, 8), 8), :]
            own = member * 32 + own_lat
            sent_ref[own] = (sent_ref[own].astype(jnp.float32) + score).astype(jnp.bfloat16)
        return 0

    lax.fori_loop(0, MEM // 2, send, 0, unroll=2)


def inverse_kernel(got_ref, table_ref, grid_hbm, score_ref, rows, grid, sems):
    own_lat = lax.axis_index("lat")
    order = message_order(64, 256)
    order = jnp.concatenate([order[g * 64 : g * 64 + 48] for g in range(GROUPS)], axis=0)
    rows[...] = got_ref[...].astype(jnp.float32).reshape(512 * 8, LANE)
    turned = []
    for t in range(4):
        pair = [rows[pl.ds(2 * t + c, 512, stride=8), :].astype(jnp.bfloat16) for c in range(2)]
        turned.append(dot(order, jnp.concatenate(pair, axis=1), ((1,), (1,))).astype(jnp.bfloat16))
    stores = []
    for h in range(2):
        left = []
        for vb in (2 * h, 2 * h + 1):
            for t in range(4):
                left.append(
                    jnp.concatenate(
                        [turned[t][g * 48 : (g + 1) * 48, vb * LANE : (vb + 1) * LANE] for g in range(GROUPS)],
                        axis=1,
                    )
                )
        result = dot(jnp.concatenate(left, axis=0), table_ref[...]).astype(jnp.bfloat16)
        for vb in range(2):
            for t in range(4):
                for k, j in enumerate((2 * t, 2 * t + 1, 8 + t)):
                    at = (vb * 4 + t) * 48 + k * VB
                    grid[0, j, h * 32 + vb * VB : h * 32 + (vb + 1) * VB, :] = result[at : at + VB]
        half = (slice(None), slice(None), slice(h * 32, (h + 1) * 32), slice(None))
        stores.append(pltpu.make_async_copy(grid.at[half], grid_hbm.at[half], sems.at[h]))
        stores[-1].start()

    slot = lax.broadcasted_iota(jnp.int32, (16, LANE), 0)
    column = lax.broadcasted_iota(jnp.int32, (16, LANE), 1) - 112
    parts = [None] * 4
    for sb in range(4):
        tile = None
        for vb in range(4):
            piece = rows[pl.ds(pl.multiple_of((vb * LANE + sb * 32 + own_lat) * 8, 8), 8), :]
            tile = piece if tile is None else tile + piece
        here = (column >= 0) & (slot == (5 * sb) // 2 + (column + 5) // 5 - 1)
        for t in range(4):
            spread = jnp.where(here, jnp.broadcast_to(tile[2 * t + 1 : 2 * t + 2], (16, LANE)), 0.0)
            parts[t] = spread if parts[t] is None else parts[t] + spread
    source = lax.broadcasted_iota(jnp.int32, (512, LANE), 0)
    target = lax.broadcasted_iota(jnp.int32, (512, LANE), 1)
    inside = source % LANE - 110
    fits = (inside >= 2) & (inside < 17) & (target == 5 * (source // LANE) + (inside + 3) % 5)
    scores = lax.dot_general(
        jnp.concatenate(parts, axis=1),
        jnp.where(fits, 1.0, 0.0),
        (((1,), (0,)), ((), ())),
        precision=lax.Precision.HIGHEST,
        preferred_element_type=jnp.float32,
    )
    score_ref[...] = scores[:10, :20] * (1.0 / 128)
    for store in stores:
        store.wait()


def body(members, analysis, wave_order):
    mib = 1 << 20
    any_spec = pl.BlockSpec(memory_space=pltpu.HBM)
    vmem_spec = pl.BlockSpec(memory_space=pltpu.VMEM)
    waves = wave_order.astype(jnp.float32)
    sent, table = pl.pallas_call(
        forward_kernel,
        in_specs=[vmem_spec, any_spec, any_spec],
        out_shape=[
            jax.ShapeDtypeStruct((512, 8, LANE), jnp.bfloat16),
            jax.ShapeDtypeStruct((640, NLON), jnp.bfloat16),
        ],
        scratch_shapes=[
            pltpu.VMEM((1, 12, 64, NLON), jnp.bfloat16),
            pltpu.VMEM((12, 64, NLON), jnp.bfloat16),
            pltpu.VMEM((2048, LANE), jnp.float32),
            pltpu.SemaphoreType.DMA((2,)),
        ],
        compiler_params=pltpu.CompilerParams(vmem_limit_bytes=60 * mib),
        cost_estimate=pl.CostEstimate(flops=3 * 10**9, bytes_accessed=4 * 10**6, transcendentals=0),
        name="forward",
    )(wave_order, members.transpose(0, 2, 1, 3), analysis.transpose(1, 0, 2))
    got = lax.all_to_all(sent, MESH_AXES, 0, 0, tiled=True)

    own = lax.axis_index("lat") * 10 + (5 * lax.rem(lax.axis_index("ens"), 4)) // 2
    slots = lax.dynamic_slice_in_dim(waves, own, 3)
    slots = jnp.concatenate([slots, jnp.broadcast_to(slots[2:3], (5,))]).reshape(8, 1)
    base = 0.5 * (
        lax.lgamma(slots + 1.5) - lax.lgamma(slots + 1.0) - lax.lgamma(jnp.float32(1.5)) + math.log(0.5)
    )
    colatitude = (latitude_order() + 0.5) * (math.pi / NLAT)
    constants = [np.cos(colatitude), np.log(np.sin(colatitude)), math.sqrt(math.pi / NLAT) * np.sin(colatitude)]
    constants = [jnp.asarray(c[None].astype(np.float32)) for c in constants]
    legendre = pl.pallas_call(
        legendre_kernel,
        out_shape=jax.ShapeDtypeStruct((DEG, 1536), jnp.bfloat16),
        scratch_shapes=[pltpu.VMEM((4, DEG * 8, LANE), jnp.float32)],
        compiler_params=pltpu.CompilerParams(vmem_limit_bytes=16 * mib),
        cost_estimate=pl.CostEstimate(flops=10**8, bytes_accessed=2 * 10**6, transcendentals=3 * 10**6),
        name="legendre",
    )(slots, base, *constants)

    sent = pl.pallas_call(
        score_kernel,
        out_shape=jax.ShapeDtypeStruct((512, 8, LANE), jnp.bfloat16),
        scratch_shapes=[
            pltpu.VMEM((GROUPS, MEM * VB, 512), jnp.bfloat16),
            pltpu.VMEM((MEM * VB, 3 * LANE), jnp.float32),
            pltpu.VMEM((GROUPS, 8, 3 * LANE), jnp.float32),
            pltpu.VMEM((LANE, LANE), jnp.float32),
        ],
        compiler_params=pltpu.CompilerParams(vmem_limit_bytes=20 * mib),
        cost_estimate=pl.CostEstimate(flops=6 * 10**9, bytes_accessed=5 * 10**6, transcendentals=5 * 10**6),
        name="score",
    )(got, legendre)
    got = lax.all_to_all(sent, MESH_AXES, 0, 0, tiled=True)

    grid_grad, coef_score = pl.pallas_call(
        inverse_kernel,
        in_specs=[vmem_spec, vmem_spec],
        out_specs=[any_spec, vmem_spec],
        out_shape=[
            jax.ShapeDtypeStruct((1, 12, 64, NLON), jnp.bfloat16),
            jax.ShapeDtypeStruct((10, 20), jnp.float32),
        ],
        scratch_shapes=[
            pltpu.VMEM((4096, LANE), jnp.float32),
            pltpu.VMEM((1, 12, 64, NLON), jnp.bfloat16),
            pltpu.SemaphoreType.DMA((2,)),
        ],
        compiler_params=pltpu.CompilerParams(vmem_limit_bytes=24 * mib),
        cost_estimate=pl.CostEstimate(flops=2 * 10**9, bytes_accessed=4 * 10**6, transcendentals=0),
        name="inverse",
    )(got, table)
    return (grid_grad.transpose(0, 2, 1, 3), coef_score)


def solution(mesh):
    placed = (P("ens", None, "lat", None), P(None, "lat", None), P())
    return jax.shard_map(
        body,
        mesh=mesh,
        in_specs=placed,
        out_specs=(P("ens", None, "lat", None), P("lat", "ens")),
        check_vma=False,
    )
```

time: 137 us -> 117 us (0.85)
  Pallas kernels: 34.3 us -> 22.7 us
  local copies, waits for them, and re-layouts: 9.66 us -> 0.85 us
    unnamed x19 -> x10, local copies, waits for them, and re-layouts: 7.24 us -> 0.03 us
    pallas_call x1, Pallas kernels: 16.1 us -> 8.9 us  [body(): pl.pallas_call(score_kernel, out_shape=jax.ShapeDtypeStruct((512, 8, LANE...]
    pallas_call x3, Pallas kernels: 18.2 us -> 13.8 us  [the longest x1 6.16 us: body(): pl.pallas_call(forward_kernel, in_specs=[vmem_spec, any_spec, any_spec],...]
  transfers between devices with their start and end apart: 1 -> 1, of which waited for: 1 -> 1; matrix products, arithmetic and copies ran while one was open for 1% -> 1% of each run, Pallas kernels for 3% -> 4%
where the time goes in v2:
time: 117 us
  blocking collectives  42.8 us (37%)
  waiting for transfers between devices  26.7 us (23%)
  Pallas kernels  22.7 us (19%)
  starting transfers between devices  22.2 us (19%)
    all_to_all x1, blocking collectives, body(): got = lax.all_to_all(sent, MESH_AXES, 0, 0, tiled=True)  42.8 us
    all_to_all x1, waiting for transfers between devices, body(): got = lax.all_to_all(sent, MESH_AXES, 0, 0, tiled=True)  26.7 us
    all_to_all x1, starting transfers between devices, body(): got = lax.all_to_all(sent, MESH_AXES, 0, 0, tiled=True)  22.2 us
    pallas_call x1, Pallas kernels, body(): pl.pallas_call(score_kernel, out_shape=jax.ShapeDtypeStruct((512, 8, LANE...  8.9 us
    pallas_call x1, Pallas kernels, body(): pl.pallas_call(forward_kernel, in_specs=[vmem_spec, any_spec, any_spec],...  6.16 us
    pallas_call x1, Pallas kernels, body(): pl.pallas_call(legendre_kernel, out_shape=jax.ShapeDtypeStruct((DEG, 1536...  4.5 us
    pallas_call x1, Pallas kernels, body(): pl.pallas_call(inverse_kernel, in_specs=[vmem_spec, vmem_spec], out_specs...  3.12 us
  transfers between devices with their start and end apart: 1, of which 1 were waited for; matrix products, arithmetic and copies ran while one was open for 1% of the time, Pallas kernels for 4%

profile of v2, /device:TPU:1, one launch (start us, length us, event | category | flops | bytes accessed | tf_op | source)
XLA Modules:
  0.0 116.7 jit_solution(11897360890109677637)
XLA Ops:
  0.6 6.2 %forward.1 = (bf16[512,8,128]{2,1,0:T(8,128)(2,1)}, bf16[640,720]{1,0:T(8,128)(2,1)}) custom-call(s32[320]{0:T(512)} %wave_ref.1, bf16[1,12,64,720]{3,2,1,0:T(8,128)(2,1)} %bitcast.8, bf16[12,64,720]{2,1,0:T(8,128)(2,1)} %bitcast.9), custom_call_target="tpu_custom_call" | custom-call | flops 3000000000 | bytes 4000000 | tf_op jit(solution)/shard_map/forward/pallas_call | solution.py:322
  6.8 0.0 copy-start.4
  6.8 0.0 copy-start
  6.8 0.0 copy-start.1
  6.8 0.0 copy-start.2
  6.8 22.2 %all-to-all-start = ((bf16[512,8,128]{2,1,0:T(8,128)(2,1)}), bf16[512,8,128]{2,1,0:T(8,128)(2,1)S(1)}, u32[]{:S(2)}, u32[]{:S(2)}) async-start(bf16[512,8,128]{2,1,0:T(8,128)(2,1)} %get-tuple-element.6), calls=%async_computation | async-start | bytes 2097152 | tf_op jit(solution)/shard_map/all_to_all | solution.py:339
  29.0 0.0 copy-done.4
  29.1 0.1 dynamic_slice.3
  29.1 0.6 slice.3
  29.7 0.7 multiply_bitcast_fusion
  30.4 0.1 copy.8.wave_ref
  30.5 0.1 copy.9.base_ref
  30.6 0.0 copy-done
  30.6 0.0 copy-done.1
  30.6 0.0 copy-done.2
  30.6 4.5 %legendre.1.leg_ref = bf16[320,1536]{1,0:T(8,128)(2,1)S(1)} custom-call(f32[8,1]{1,0:T(8,128)S(1)} %copy.8.wave_ref, f32[8,1]{1,0:T(8,128)S(1)} %copy.9.base_ref, f32[1,512]{1,0:T(1,128)S(1)} %copy-done, f32[1,512]{1,0:T(1,128)S(1)} %copy-done.1, f32[1,512]{1,0:T(1,128)S(1)} %copy-done.2), custom_call_target="tpu_custom_call" | custom-call | flops 100000000 | bytes 2000000 | tf_op jit(solution)/shard_map/legendre/pallas_call | solution.py:350
  35.1 26.7 %all-to-all-done.got_ref = bf16[512,8,128]{2,1,0:T(8,128)(2,1)S(1)} async-done(((bf16[512,8,128]{2,1,0:T(8,128)(2,1)}), bf16[512,8,128]{2,1,0:T(8,128)(2,1)S(1)}, u32[]{:S(2)}, u32[]{:S(2)}) %all-to-all-start) | async-done | bytes 1048608 | tf_op jit(solution)/shard_map/all_to_all | solution.py:339
  61.9 8.9 %score.1 = bf16[512,8,128]{2,1,0:T(8,128)(2,1)S(1)} custom-call(bf16[512,8,128]{2,1,0:T(8,128)(2,1)S(1)} %all-to-all-done.got_ref, bf16[320,1536]{1,0:T(8,128)(2,1)S(1)} %legendre.1.leg_ref), custom_call_target="tpu_custom_call" | custom-call | flops 6000000000 | bytes 5000000 | tf_op jit(solution)/shard_map/score/pallas_call | solution.py:359
  70.8 0.0 copy-start.3
  70.8 42.8 %all_to_all.10.got_ref = bf16[512,8,128]{2,1,0:T(8,128)(2,1)S(1)} all-to-all(bf16[512,8,128]{2,1,0:T(8,128)(2,1)S(1)} %score.1), channel_id=1, replica_groups=mesh['ens'=16,'lat'=32] {'ens','lat'}, dimensions={0} | all-to-all | bytes 2097152 | tf_op jit(solution)/shard_map/all_to_all | solution.py:372
  113.6 0.0 copy-done.3
  113.6 3.1 %inverse.1 = (bf16[1,12,64,720]{3,2,1,0:T(8,128)(2,1)}, f32[10,20]{1,0:T(8,128)}) custom-call(bf16[512,8,128]{2,1,0:T(8,128)(2,1)S(1)} %all_to_all.10.got_ref, bf16[640,720]{1,0:T(8,128)(2,1)S(1)} %copy-done.3), custom_call_target="tpu_custom_call" | custom-call | flops 2000000000 | bytes 4000000 | tf_op jit(solution)/shard_map/inverse/pallas_call | solution.py:374
  (1 shorter events, 0.0 us)
Async XLA Ops:
  6.8 22.2 %copy-start.4 = (s32[320]{0:T(512)S(1)}, s32[320]{0:T(512)}, u32[]{:S(2)}) copy-start(s32[320]{0:T(512)} %wave_ref.1) | copy-start | bytes 3844
  6.8 23.8 %copy-start = (f32[1,512]{1,0:T(1,128)S(1)}, f32[1,512]{1,0:T(1,128)}, u32[]{:S(2)}) copy-start(f32[1,512]{1,0:T(1,128)} %constant.112.clone.cos_ref) | copy-start | bytes 6148
  6.8 23.8 %copy-start.1 = (f32[1,512]{1,0:T(1,128)S(1)}, f32[1,512]{1,0:T(1,128)}, u32[]{:S(2)}) copy-start(f32[1,512]{1,0:T(1,128)} %constant.113.clone.logsin_ref) | copy-start | bytes 6148
  6.8 23.8 %copy-start.2 = (f32[1,512]{1,0:T(1,128)S(1)}, f32[1,512]{1,0:T(1,128)}, u32[]{:S(2)}) copy-start(f32[1,512]{1,0:T(1,128)} %constant.114.clone.weight_ref) | copy-start | bytes 6148
  6.8 55.0 %all-to-all-start = ((bf16[512,8,128]{2,1,0:T(8,128)(2,1)}), bf16[512,8,128]{2,1,0:T(8,128)(2,1)S(1)}, u32[]{:S(2)}, u32[]{:S(2)}) async-start(bf16[512,8,128]{2,1,0:T(8,128)(2,1)} %get-tuple-element.6), calls=%async_computation | async-start | bytes 2097152 | tf_op jit(solution)/shard_map/all_to_all | solution.py:339
  70.8 42.9 %copy-start.3 = (bf16[640,720]{1,0:T(8,128)(2,1)S(1)}, bf16[640,720]{1,0:T(8,128)(2,1)}, u32[]{:S(2)}) copy-start(bf16[640,720]{1,0:T(8,128)(2,1)} %get-tuple-element.7.table_ref) | copy-start | bytes 2764804

commit v3 on v2

--- a/solution.py
+++ b/solution.py
@@ -18,18 +18,17 @@
 MESH_AXES = ("ens", "lat")
 
 
-def message_order(rows, width):
-    shape = (GROUPS * rows, width)
-    row = lax.broadcasted_iota(jnp.int32, shape, 0)
-    lane = lax.broadcasted_iota(jnp.int32, shape, 1)
-    g, inner = row // rows, row % rows
-    k, v = inner % 64 // VB, row % VB
-    second = jnp.where(g >= 3, 1, 0)
-    plain = k * LANE + 16 * g + v
-    extra = second * LANE + 80 + 16 * (g - 3 * second) + v
-    place = jnp.where(k < 2, plain, jnp.where(k == 2, extra, -1024))
-    place = place + 256 * (inner // 64)
-    return jnp.where(place == lane, 1.0, 0.0).astype(jnp.bfloat16)
+def message_order(columns):
+    row = lax.broadcasted_iota(jnp.int32, (LANE, LANE), 0)
+    lane = lax.broadcasted_iota(jnp.int32, (LANE, LANE), 1)
+    k, ahead = (row >> 4) & 3, (row & 15) - lane + 256 * (row >> 6)
+    groups = []
+    for g in range(GROUPS):
+        extra = 80 if g < 3 else 160
+        place = ahead + 16 * g + jnp.where(k < 2, k * LANE, jnp.where(k == 2, extra, -2048))
+        tiles = [jnp.where(place == q * LANE, 1.0, 0.0) for q in range(columns)]
+        groups.append(jnp.concatenate(tiles, axis=1).astype(jnp.bfloat16))
+    return groups
 
 
 def latitude_order():
@@ -42,19 +41,24 @@
     return lax.dot_general(a, b, (dims, ((), ())), preferred_element_type=jnp.float32)
 
 
-SIN_TERMS = [(-1) ** n / math.factorial(2 * n + 1) for n in range(7)]
-
-
-def fourier_block(wave, part):
+STEP = math.pi / 360.0
+SIN_TERMS = [(-1) ** n / math.factorial(2 * n + 1) * STEP ** (2 * n + 1) / math.sqrt(NLON) for n in range(6)]
+
+
+def scaled_sine(steps):
+    square = steps * steps
+    total = SIN_TERMS[5]
+    for term in SIN_TERMS[4::-1]:
+        total = total * square + term
+    return (total * steps).astype(jnp.bfloat16)
+
+
+def fourier_blocks(wave):
     lon = lax.broadcasted_iota(jnp.int32, (32, NLON), 1).astype(jnp.float32)
-    turn = wave * lon + 180.0 * part
-    turn = turn - NLON * jnp.floor((turn + 0.5) * (1.0 / NLON))
-    x = (jnp.abs(turn - 360.0) - 180.0) * (math.pi / 360.0)
-    x2 = x * x
-    total = SIN_TERMS[6]
-    for term in SIN_TERMS[5::-1]:
-        total = total * x2 + term
-    return total * x * (1.0 / math.sqrt(NLON))
+    turn = wave * lon
+    turn = turn - NLON * jnp.floor((turn + 0.5) * (1.0 / NLON)) - 360.0
+    folded = jnp.maximum(jnp.minimum(turn, 360.0 - turn), -360.0 - turn)
+    return scaled_sine(jnp.abs(turn) - 180.0), scaled_sine(folded)
 
 
 def forward_kernel(wave_ref, members_hbm, analysis_hbm, sent_ref, table_ref, members, analysis, rows, sems):
@@ -67,12 +71,12 @@
     waves = jnp.broadcast_to(wave_ref[...].reshape(1, DEG).astype(jnp.float32), (32, DEG))
     ahead = lax.broadcasted_iota(jnp.int32, (32, DEG), 1) - 10 * lax.broadcasted_iota(jnp.int32, (32, DEG), 0)
     columns = [jnp.sum(jnp.where(ahead == k, waves, 0.0), axis=1, keepdims=True) for k in range(10)]
-    for g in range(GROUPS):
-        for sb in range(4):
-            pair = 5 * sb + g
+    for slot in range(10):
+        for part, block in enumerate(fourier_blocks(columns[slot])):
+            sb, g = divmod(2 * slot + part, GROUPS)
             at = g * LANE + sb * 32
-            table_ref[at : at + 32, :] = fourier_block(columns[pair // 2], pair % 2).astype(jnp.bfloat16)
-    order = message_order(LANE, 512)
+            table_ref[at : at + 32, :] = block
+    order = jnp.concatenate(message_order(4), axis=0)
     for load in loads:
         load.wait()
 
@@ -169,7 +173,7 @@
 def score_kernel(got_ref, leg_ref, sent_ref, turned, coef, sums, scores):
     own_lat = lax.axis_index("lat")
     odd_block = lax.rem(lax.axis_index("ens"), 2)
-    even = lax.rem(lax.broadcasted_iota(jnp.int32, (48, 256), 1), 2) == 0
+    even = lax.broadcasted_iota(jnp.int32, (48, 256), 1) & 1 == 0
     unit = lax.broadcasted_iota(jnp.int32, (256, 256), 0) == lax.broadcasted_iota(jnp.int32, (256, 256), 1)
     unit = jnp.where(unit, 1.0, 0.0).astype(jnp.bfloat16)
 
@@ -193,41 +197,50 @@
 
     first_half = lax.broadcasted_iota(jnp.int32, (8, LANE), 1) < 64
 
-    def group(g, _):
-        spectra = dot(turned[g], leg_ref[:, slot_lanes(g)], ((1,), (1,)))
-        coef[:, 0:DEG] = spectra.astype(jnp.bfloat16).astype(jnp.float32)
+    def spectra(g):
+        values = dot(turned[g], leg_ref[:, slot_lanes(g)], ((1,), (1,)))
+        coef[g, :, 0:DEG] = values.astype(jnp.bfloat16).astype(jnp.float32)
+
+    def score(g):
         for q in range(2):
             lanes = slice(q * LANE, (q + 1) * LANE)
             total = None
             for r in range(2):
-                grads, per = pair_terms([coef[e * VB + r * 8 : e * VB + r * 8 + 8, lanes] for e in range(MEM)])
-                for e in range(MEM):
-                    coef[e * VB + r * 8 : e * VB + r * 8 + 8, lanes] = grads[e]
+                rows = [slice(e * VB + r * 8, e * VB + r * 8 + 8) for e in range(MEM)]
+                grads, per = pair_terms([coef[g, row, lanes] for row in rows])
+                for row, grad in zip(rows, grads):
+                    coef[g, row, lanes] = grad
                 total = per if total is None else total + per
             sums[g, :, lanes] = total
         lanes = slice(2 * LANE, 3 * LANE)
         packed = []
         for e in range(MEM):
-            top, bottom = coef[e * VB : e * VB + 8, lanes], coef[e * VB + 8 : e * VB + VB, lanes]
+            top, bottom = coef[g, e * VB : e * VB + 8, lanes], coef[g, e * VB + 8 : e * VB + VB, lanes]
             packed.append(jnp.where(first_half, top, pltpu.roll(bottom, 64, 1)))
         grads, per = pair_terms(packed)
         for e in range(MEM):
-            coef[e * VB : e * VB + 8, lanes] = grads[e]
-            coef[e * VB + 8 : e * VB + VB, lanes] = pltpu.roll(grads[e], 64, 1)
+            coef[g, e * VB : e * VB + 8, lanes] = grads[e]
+            coef[g, e * VB + 8 : e * VB + VB, lanes] = pltpu.roll(grads[e], 64, 1)
         sums[g, :, lanes] = per + pltpu.roll(per, 64, 1)
-        grad = coef[:, 0:DEG].astype(jnp.bfloat16)
+
+    def gradient(g):
+        grad = coef[g, :, 0:DEG].astype(jnp.bfloat16)
         turned[g] = dot(grad, leg_ref[:, slot_lanes(g)]).astype(jnp.bfloat16)
-        return 0
-
-    lax.fori_loop(0, GROUPS, group, 0)
+
+    spectra(0)
+    for g in range(GROUPS):
+        if g + 1 < GROUPS:
+            spectra(g + 1)
+        score(g)
+        gradient(g)
 
     place = lax.broadcasted_iota(jnp.int32, (16, DEG), 0)
     same = lax.rem(lax.broadcasted_iota(jnp.int32, (16, DEG), 1), 5) == lax.rem(place, 5)
     spread = jnp.zeros((16, DEG), jnp.float32)
     for g in range(GROUPS):
         mine = same & (place < 15) & (place // 5 == (g + odd_block) // 2)
-        score = jnp.sum(sums[g], axis=0, keepdims=True)[:, 0:DEG]
-        spread = spread + jnp.where(mine, jnp.broadcast_to(score, (16, DEG)), 0.0)
+        own = jnp.sum(sums[g], axis=0, keepdims=True)[:, 0:DEG]
+        spread = spread + jnp.where(mine, jnp.broadcast_to(own, (16, DEG)), 0.0)
     spread = jnp.concatenate([jnp.zeros((112, DEG), jnp.float32), spread], axis=0).astype(jnp.bfloat16)
     out_row = lax.broadcasted_iota(jnp.int32, (LANE, DEG), 0)
     out_deg = lax.broadcasted_iota(jnp.int32, (LANE, DEG), 1)
@@ -248,9 +261,9 @@
             member = 2 * pair + k
             message = back[:, k * LANE : (k + 1) * LANE].reshape(32, 8, LANE)
             sent_ref[pl.ds(pl.multiple_of(member * 32, 32), 32)] = message.astype(jnp.bfloat16)
-            score = scores[pl.ds(pl.multiple_of(member * 8, 8), 8), :]
+            part = scores[pl.ds(pl.multiple_of(member * 8, 8), 8), :]
             own = member * 32 + own_lat
-            sent_ref[own] = (sent_ref[own].astype(jnp.float32) + score).astype(jnp.bfloat16)
+            sent_ref[own] = (sent_ref[own].astype(jnp.float32) + part).astype(jnp.bfloat16)
         return 0
 
     lax.fori_loop(0, MEM // 2, send, 0, unroll=2)
@@ -258,8 +271,7 @@
 
 def inverse_kernel(got_ref, table_ref, grid_hbm, score_ref, rows, grid, sems):
     own_lat = lax.axis_index("lat")
-    order = message_order(64, 256)
-    order = jnp.concatenate([order[g * 64 : g * 64 + 48] for g in range(GROUPS)], axis=0)
+    order = jnp.concatenate([group[0:48] for group in message_order(2)], axis=0)
     rows[...] = got_ref[...].astype(jnp.float32).reshape(512 * 8, LANE)
     turned = []
     for t in range(4):
@@ -361,7 +373,7 @@
         out_shape=jax.ShapeDtypeStruct((512, 8, LANE), jnp.bfloat16),
         scratch_shapes=[
             pltpu.VMEM((GROUPS, MEM * VB, 512), jnp.bfloat16),
-            pltpu.VMEM((MEM * VB, 3 * LANE), jnp.float32),
+            pltpu.VMEM((GROUPS, MEM * VB, 3 * LANE), jnp.float32),
             pltpu.VMEM((GROUPS, 8, 3 * LANE), jnp.float32),
             pltpu.VMEM((LANE, LANE), jnp.float32),
         ],

time: 117 us -> 115 us (0.983)
  Pallas kernels: 22.7 us -> 20.4 us
    pallas_call x1, Pallas kernels: 8.9 us -> 7.34 us  [body(): pl.pallas_call(score_kernel, out_shape=jax.ShapeDtypeStruct((512, 8, LANE...]
where the time goes in v3:
time: 115 us
  blocking collectives  43 us (37%)
  waiting for transfers between devices  26.7 us (23%)
  starting transfers between devices  22.2 us (19%)
  Pallas kernels  20.4 us (18%)
    all_to_all x1, blocking collectives, body(): got = lax.all_to_all(sent, MESH_AXES, 0, 0, tiled=True)  43 us
    all_to_all x1, waiting for transfers between devices, body(): got = lax.all_to_all(sent, MESH_AXES, 0, 0, tiled=True)  26.7 us
    all_to_all x1, starting transfers between devices, body(): got = lax.all_to_all(sent, MESH_AXES, 0, 0, tiled=True)  22.2 us
    pallas_call x1, Pallas kernels, body(): pl.pallas_call(score_kernel, out_shape=jax.ShapeDtypeStruct((512, 8, LANE...  7.34 us
    pallas_call x1, Pallas kernels, body(): pl.pallas_call(forward_kernel, in_specs=[vmem_spec, any_spec, any_spec],...  5.51 us
    pallas_call x1, Pallas kernels, body(): pl.pallas_call(legendre_kernel, out_shape=jax.ShapeDtypeStruct((DEG, 1536...  4.5 us
    pallas_call x1, Pallas kernels, body(): pl.pallas_call(inverse_kernel, in_specs=[vmem_spec, vmem_spec], out_specs...  3.09 us
  transfers between devices with their start and end apart: 1, of which 1 were waited for; matrix products, arithmetic and copies ran while one was open for 1% of the time, Pallas kernels for 4%

profile of v3, /device:TPU:1, one launch (start us, length us, event | category | flops | bytes accessed | tf_op | source)
XLA Modules:
  0.0 114.9 jit_solution(12400856678561723272)
XLA Ops:
  0.6 5.5 %forward.1 = (bf16[512,8,128]{2,1,0:T(8,128)(2,1)}, bf16[640,720]{1,0:T(8,128)(2,1)}) custom-call(s32[320]{0:T(512)} %wave_ref.1, bf16[1,12,64,720]{3,2,1,0:T(8,128)(2,1)} %bitcast.8, bf16[12,64,720]{2,1,0:T(8,128)(2,1)} %bitcast.9), custom_call_target="tpu_custom_call" | custom-call | flops 3000000000 | bytes 4000000 | tf_op jit(solution)/shard_map/forward/pallas_call | solution.py:334
  6.1 0.0 copy-start.4
  6.2 0.0 copy-start
  6.2 0.0 copy-start.1
  6.2 0.0 copy-start.2
  6.2 22.2 %all-to-all-start = ((bf16[512,8,128]{2,1,0:T(8,128)(2,1)}), bf16[512,8,128]{2,1,0:T(8,128)(2,1)S(1)}, u32[]{:S(2)}, u32[]{:S(2)}) async-start(bf16[512,8,128]{2,1,0:T(8,128)(2,1)} %get-tuple-element.6), calls=%async_computation | async-start | bytes 2097152 | tf_op jit(solution)/shard_map/all_to_all | solution.py:351
  28.4 0.0 copy-done.4
  28.4 0.1 dynamic_slice.3
  28.5 0.6 slice.3
  29.1 0.7 multiply_bitcast_fusion
  29.8 0.1 copy.8.wave_ref
  29.9 0.1 copy.9.base_ref
  30.0 0.0 copy-done
  30.0 0.0 copy-done.1
  30.0 0.0 copy-done.2
  30.0 4.5 %legendre.1.leg_ref = bf16[320,1536]{1,0:T(8,128)(2,1)S(1)} custom-call(f32[8,1]{1,0:T(8,128)S(1)} %copy.8.wave_ref, f32[8,1]{1,0:T(8,128)S(1)} %copy.9.base_ref, f32[1,512]{1,0:T(1,128)S(1)} %copy-done, f32[1,512]{1,0:T(1,128)S(1)} %copy-done.1, f32[1,512]{1,0:T(1,128)S(1)} %copy-done.2), custom_call_target="tpu_custom_call" | custom-call | flops 100000000 | bytes 2000000 | tf_op jit(solution)/shard_map/legendre/pallas_call | solution.py:362
  34.5 26.7 %all-to-all-done.got_ref = bf16[512,8,128]{2,1,0:T(8,128)(2,1)S(1)} async-done(((bf16[512,8,128]{2,1,0:T(8,128)(2,1)}), bf16[512,8,128]{2,1,0:T(8,128)(2,1)S(1)}, u32[]{:S(2)}, u32[]{:S(2)}) %all-to-all-start) | async-done | bytes 1048608 | tf_op jit(solution)/shard_map/all_to_all | solution.py:351
  61.2 7.3 %score.1 = bf16[512,8,128]{2,1,0:T(8,128)(2,1)S(1)} custom-call(bf16[512,8,128]{2,1,0:T(8,128)(2,1)S(1)} %all-to-all-done.got_ref, bf16[320,1536]{1,0:T(8,128)(2,1)S(1)} %legendre.1.leg_ref), custom_call_target="tpu_custom_call" | custom-call | flops 6000000000 | bytes 5000000 | tf_op jit(solution)/shard_map/score/pallas_call | solution.py:371
  68.6 0.0 copy-start.3
  68.6 43.0 %all_to_all.10.got_ref = bf16[512,8,128]{2,1,0:T(8,128)(2,1)S(1)} all-to-all(bf16[512,8,128]{2,1,0:T(8,128)(2,1)S(1)} %score.1), channel_id=1, replica_groups=mesh['ens'=16,'lat'=32] {'ens','lat'}, dimensions={0} | all-to-all | bytes 2097152 | tf_op jit(solution)/shard_map/all_to_all | solution.py:384
  111.6 0.0 copy-done.3
  111.6 3.1 %inverse.1 = (bf16[1,12,64,720]{3,2,1,0:T(8,128)(2,1)}, f32[10,20]{1,0:T(8,128)}) custom-call(bf16[512,8,128]{2,1,0:T(8,128)(2,1)S(1)} %all_to_all.10.got_ref, bf16[640,720]{1,0:T(8,128)(2,1)S(1)} %copy-done.3), custom_call_target="tpu_custom_call" | custom-call | flops 2000000000 | bytes 4000000 | tf_op jit(solution)/shard_map/inverse/pallas_call | solution.py:386
  (1 shorter events, 0.0 us)
Async XLA Ops:
  6.1 22.2 %copy-start.4 = (s32[320]{0:T(512)S(1)}, s32[320]{0:T(512)}, u32[]{:S(2)}) copy-start(s32[320]{0:T(512)} %wave_ref.1) | copy-start | bytes 3844
  6.2 23.8 %copy-start = (f32[1,512]{1,0:T(1,128)S(1)}, f32[1,512]{1,0:T(1,128)}, u32[]{:S(2)}) copy-start(f32[1,512]{1,0:T(1,128)} %constant.112.clone.cos_ref) | copy-start | bytes 6148
  6.2 23.8 %copy-start.1 = (f32[1,512]{1,0:T(1,128)S(1)}, f32[1,512]{1,0:T(1,128)}, u32[]{:S(2)}) copy-start(f32[1,512]{1,0:T(1,128)} %constant.113.clone.logsin_ref) | copy-start | bytes 6148
  6.2 23.8 %copy-start.2 = (f32[1,512]{1,0:T(1,128)S(1)}, f32[1,512]{1,0:T(1,128)}, u32[]{:S(2)}) copy-start(f32[1,512]{1,0:T(1,128)} %constant.114.clone.weight_ref) | copy-start | bytes 6148
  6.2 55.0 %all-to-all-start = ((bf16[512,8,128]{2,1,0:T(8,128)(2,1)}), bf16[512,8,128]{2,1,0:T(8,128)(2,1)S(1)}, u32[]{:S(2)}, u32[]{:S(2)}) async-start(bf16[512,8,128]{2,1,0:T(8,128)(2,1)} %get-tuple-element.6), calls=%async_computation | async-start | bytes 2097152 | tf_op jit(solution)/shard_map/all_to_all | solution.py:351
  68.6 43.0 %copy-start.3 = (bf16[640,720]{1,0:T(8,128)(2,1)S(1)}, bf16[640,720]{1,0:T(8,128)(2,1)}, u32[]{:S(2)}) copy-start(bf16[640,720]{1,0:T(8,128)(2,1)} %get-tuple-element.7.table_ref) | copy-start | bytes 2764804

commit v4 on v3

--- a/solution.py
+++ b/solution.py
@@ -102,10 +102,10 @@
         for t in range(4):
             for q in range(4):
                 at = (q // 2) * LANE * 8 + 2 * t + q % 2
-                rows[pl.ds(at, LANE, stride=8), :] = placed[
+                rows[h, pl.ds(at, LANE, stride=8), :] = placed[
                     t * LANE : (t + 1) * LANE, q * LANE : (q + 1) * LANE
                 ]
-        sent_ref[h * 256 : (h + 1) * 256] = rows[...].reshape(256, 8, LANE).astype(jnp.bfloat16)
+        sent_ref[h * 256 : (h + 1) * 256] = rows[h].reshape(256, 8, LANE).astype(jnp.bfloat16)
 
 
 def legendre_kernel(wave_ref, base_ref, cos_ref, logsin_ref, weight_ref, leg_ref, rows):
@@ -193,7 +193,7 @@
             turned[g, at, 256:512] = extra
         return 0
 
-    lax.fori_loop(0, MEM, turn, 0, unroll=4)
+    lax.fori_loop(0, MEM, turn, 0, unroll=True)
 
     first_half = lax.broadcasted_iota(jnp.int32, (8, LANE), 1) < 64
 
@@ -266,7 +266,7 @@
             sent_ref[own] = (sent_ref[own].astype(jnp.float32) + part).astype(jnp.bfloat16)
         return 0
 
-    lax.fori_loop(0, MEM // 2, send, 0, unroll=2)
+    lax.fori_loop(0, MEM // 2, send, 0, unroll=True)
 
 
 def inverse_kernel(got_ref, table_ref, grid_hbm, score_ref, rows, grid, sems):
@@ -341,7 +341,7 @@
         scratch_shapes=[
             pltpu.VMEM((1, 12, 64, NLON), jnp.bfloat16),
             pltpu.VMEM((12, 64, NLON), jnp.bfloat16),
-            pltpu.VMEM((2048, LANE), jnp.float32),
+            pltpu.VMEM((2, 2048, LANE), jnp.float32),
             pltpu.SemaphoreType.DMA((2,)),
         ],
         compiler_params=pltpu.CompilerParams(vmem_limit_bytes=60 * mib),

time: 115 us -> 113 us (0.983)
  Pallas kernels: 20.4 us -> 18.9 us
    pallas_call x1, Pallas kernels: 7.34 us -> 5.84 us  [body(): pl.pallas_call(score_kernel, out_shape=jax.ShapeDtypeStruct((512, 8, LANE...]
where the time goes in v4:
time: 113 us
  blocking collectives  42.8 us (38%)
  waiting for transfers between devices  26.7 us (24%)
  starting transfers between devices  22.2 us (20%)
  Pallas kernels  18.9 us (17%)
    all_to_all x1, blocking collectives, body(): got = lax.all_to_all(sent, MESH_AXES, 0, 0, tiled=True)  42.8 us
    all_to_all x1, waiting for transfers between devices, body(): got = lax.all_to_all(sent, MESH_AXES, 0, 0, tiled=True)  26.7 us
    all_to_all x1, starting transfers between devices, body(): got = lax.all_to_all(sent, MESH_AXES, 0, 0, tiled=True)  22.2 us
    pallas_call x1, Pallas kernels, body(): pl.pallas_call(score_kernel, out_shape=jax.ShapeDtypeStruct((512, 8, LANE...  5.84 us
    pallas_call x1, Pallas kernels, body(): pl.pallas_call(forward_kernel, in_specs=[vmem_spec, any_spec, any_spec],...  5.51 us
    pallas_call x1, Pallas kernels, body(): pl.pallas_call(legendre_kernel, out_shape=jax.ShapeDtypeStruct((DEG, 1536...  4.5 us
    pallas_call x1, Pallas kernels, body(): pl.pallas_call(inverse_kernel, in_specs=[vmem_spec, vmem_spec], out_specs...  3.09 us
  transfers between devices with their start and end apart: 1, of which 1 were waited for; matrix products, arithmetic and copies ran while one was open for 1% of the time, Pallas kernels for 4%

profile of v4, /device:TPU:1, one launch (start us, length us, event | category | flops | bytes accessed | tf_op | source)
XLA Modules:
  0.0 113.2 jit_solution(17773560463932423525)
XLA Ops:
  0.6 5.5 %forward.1 = (bf16[512,8,128]{2,1,0:T(8,128)(2,1)}, bf16[640,720]{1,0:T(8,128)(2,1)}) custom-call(s32[320]{0:T(512)} %wave_ref.1, bf16[1,12,64,720]{3,2,1,0:T(8,128)(2,1)} %bitcast.8, bf16[12,64,720]{2,1,0:T(8,128)(2,1)} %bitcast.9), custom_call_target="tpu_custom_call" | custom-call | flops 3000000000 | bytes 4000000 | tf_op jit(solution)/shard_map/forward/pallas_call | solution.py:334
  6.1 0.0 copy-start.4
  6.2 0.0 copy-start
  6.2 0.0 copy-start.1
  6.2 0.0 copy-start.2
  6.2 22.2 %all-to-all-start = ((bf16[512,8,128]{2,1,0:T(8,128)(2,1)}), bf16[512,8,128]{2,1,0:T(8,128)(2,1)S(1)}, u32[]{:S(2)}, u32[]{:S(2)}) async-start(bf16[512,8,128]{2,1,0:T(8,128)(2,1)} %get-tuple-element.6), calls=%async_computation | async-start | bytes 2097152 | tf_op jit(solution)/shard_map/all_to_all | solution.py:351
  28.4 0.0 copy-done.4
  28.4 0.1 dynamic_slice.3
  28.5 0.6 slice.3
  29.1 0.7 multiply_bitcast_fusion
  29.8 0.1 copy.8.wave_ref
  29.9 0.1 copy.9.base_ref
  30.0 0.0 copy-done
  30.0 0.0 copy-done.1
  30.0 0.0 copy-done.2
  30.0 4.5 %legendre.1.leg_ref = bf16[320,1536]{1,0:T(8,128)(2,1)S(1)} custom-call(f32[8,1]{1,0:T(8,128)S(1)} %copy.8.wave_ref, f32[8,1]{1,0:T(8,128)S(1)} %copy.9.base_ref, f32[1,512]{1,0:T(1,128)S(1)} %copy-done, f32[1,512]{1,0:T(1,128)S(1)} %copy-done.1, f32[1,512]{1,0:T(1,128)S(1)} %copy-done.2), custom_call_target="tpu_custom_call" | custom-call | flops 100000000 | bytes 2000000 | tf_op jit(solution)/shard_map/legendre/pallas_call | solution.py:362
  34.5 26.7 %all-to-all-done.got_ref = bf16[512,8,128]{2,1,0:T(8,128)(2,1)S(1)} async-done(((bf16[512,8,128]{2,1,0:T(8,128)(2,1)}), bf16[512,8,128]{2,1,0:T(8,128)(2,1)S(1)}, u32[]{:S(2)}, u32[]{:S(2)}) %all-to-all-start) | async-done | bytes 1048608 | tf_op jit(solution)/shard_map/all_to_all | solution.py:351
  61.2 5.8 %score.1 = bf16[512,8,128]{2,1,0:T(8,128)(2,1)S(1)} custom-call(bf16[512,8,128]{2,1,0:T(8,128)(2,1)S(1)} %all-to-all-done.got_ref, bf16[320,1536]{1,0:T(8,128)(2,1)S(1)} %legendre.1.leg_ref), custom_call_target="tpu_custom_call" | custom-call | flops 6000000000 | bytes 5000000 | tf_op jit(solution)/shard_map/score/pallas_call | solution.py:371
  67.1 0.0 copy-start.3
  67.1 42.8 %all_to_all.10.got_ref = bf16[512,8,128]{2,1,0:T(8,128)(2,1)S(1)} all-to-all(bf16[512,8,128]{2,1,0:T(8,128)(2,1)S(1)} %score.1), channel_id=1, replica_groups=mesh['ens'=16,'lat'=32] {'ens','lat'}, dimensions={0} | all-to-all | bytes 2097152 | tf_op jit(solution)/shard_map/all_to_all | solution.py:384
  109.9 0.0 copy-done.3
  109.9 3.1 %inverse.1 = (bf16[1,12,64,720]{3,2,1,0:T(8,128)(2,1)}, f32[10,20]{1,0:T(8,128)}) custom-call(bf16[512,8,128]{2,1,0:T(8,128)(2,1)S(1)} %all_to_all.10.got_ref, bf16[640,720]{1,0:T(8,128)(2,1)S(1)} %copy-done.3), custom_call_target="tpu_custom_call" | custom-call | flops 2000000000 | bytes 4000000 | tf_op jit(solution)/shard_map/inverse/pallas_call | solution.py:386
  (1 shorter events, 0.0 us)
Async XLA Ops:
  6.1 22.2 %copy-start.4 = (s32[320]{0:T(512)S(1)}, s32[320]{0:T(512)}, u32[]{:S(2)}) copy-start(s32[320]{0:T(512)} %wave_ref.1) | copy-start | bytes 3844
  6.2 23.8 %copy-start = (f32[1,512]{1,0:T(1,128)S(1)}, f32[1,512]{1,0:T(1,128)}, u32[]{:S(2)}) copy-start(f32[1,512]{1,0:T(1,128)} %constant.112.clone.cos_ref) | copy-start | bytes 6148
  6.2 23.8 %copy-start.1 = (f32[1,512]{1,0:T(1,128)S(1)}, f32[1,512]{1,0:T(1,128)}, u32[]{:S(2)}) copy-start(f32[1,512]{1,0:T(1,128)} %constant.113.clone.logsin_ref) | copy-start | bytes 6148
  6.2 23.8 %copy-start.2 = (f32[1,512]{1,0:T(1,128)S(1)}, f32[1,512]{1,0:T(1,128)}, u32[]{:S(2)}) copy-start(f32[1,512]{1,0:T(1,128)} %constant.114.clone.weight_ref) | copy-start | bytes 6148
  6.2 55.0 %all-to-all-start = ((bf16[512,8,128]{2,1,0:T(8,128)(2,1)}), bf16[512,8,128]{2,1,0:T(8,128)(2,1)S(1)}, u32[]{:S(2)}, u32[]{:S(2)}) async-start(bf16[512,8,128]{2,1,0:T(8,128)(2,1)} %get-tuple-element.6), calls=%async_computation | async-start | bytes 2097152 | tf_op jit(solution)/shard_map/all_to_all | solution.py:351
  67.1 42.9 %copy-start.3 = (bf16[640,720]{1,0:T(8,128)(2,1)S(1)}, bf16[640,720]{1,0:T(8,128)(2,1)}, u32[]{:S(2)}) copy-start(bf16[640,720]{1,0:T(8,128)(2,1)} %get-tuple-element.7.table_ref) | copy-start | bytes 2764804

commit v5 on v4

--- a/solution.py
+++ b/solution.py
@@ -61,7 +61,9 @@
     return scaled_sine(jnp.abs(turn) - 180.0), scaled_sine(folded)
 
 
-def forward_kernel(wave_ref, members_hbm, analysis_hbm, sent_ref, table_ref, members, analysis, rows, sems):
+def forward_kernel(
+    wave_ref, members_hbm, analysis_hbm, sent_hbm, table_hbm, members, analysis, rows, sent_ref, table_ref, sems
+):
     loads = [
         pltpu.make_async_copy(members_hbm, members, sems.at[0]),
         pltpu.make_async_copy(analysis_hbm, analysis, sems.at[1]),
@@ -76,11 +78,15 @@
             sb, g = divmod(2 * slot + part, GROUPS)
             at = g * LANE + sb * 32
             table_ref[at : at + 32, :] = block
+    stores = [pltpu.make_async_copy(table_ref, table_hbm, sems.at[2])]
+    stores[0].start()
     order = jnp.concatenate(message_order(4), axis=0)
     for load in loads:
         load.wait()
 
-    deviation = (members[0].astype(jnp.float32) - analysis[...].astype(jnp.float32)).astype(jnp.bfloat16)
+    deviation = (members[0].astype(jnp.float32) - analysis[...].astype(jnp.float32)).astype(
+        jnp.bfloat16
+    )
     blank = jnp.zeros((VB, NLON), jnp.bfloat16)
     for h in range(2):
         pieces = []
@@ -106,6 +112,11 @@
                     t * LANE : (t + 1) * LANE, q * LANE : (q + 1) * LANE
                 ]
         sent_ref[h * 256 : (h + 1) * 256] = rows[h].reshape(256, 8, LANE).astype(jnp.bfloat16)
+        half = pl.ds(h * 256, 256)
+        stores.append(pltpu.make_async_copy(sent_ref.at[half], sent_hbm.at[half], sems.at[3 + h]))
+        stores[-1].start()
+    for store in stores:
+        store.wait()
 
 
 def legendre_kernel(wave_ref, base_ref, cos_ref, logsin_ref, weight_ref, leg_ref, rows):
@@ -180,20 +191,24 @@
     def slot_lanes(g):
         return pl.ds(pl.multiple_of((g + odd_block) // 2 * 512, 512), 512)
 
-    def turn(member, _):
-        message = got_ref[pl.ds(pl.multiple_of(member * 32, 32), 32)].astype(jnp.float32)
-        message = message.reshape(256, LANE).astype(jnp.bfloat16)
-        rows = dot(unit[:LANE, :LANE], message, ((1,), (1,)))
-        at = pl.ds(pl.multiple_of(member * VB, VB), VB)
-        low = jnp.where(even, rows[80:128], 0.0).astype(jnp.bfloat16)
-        high = jnp.where(even, 0.0, rows[80:128]).astype(jnp.bfloat16)
-        for g in range(GROUPS):
-            turned[g, at, 0:256] = rows[g * VB : (g + 1) * VB].astype(jnp.bfloat16)
-            extra = low[g * VB : (g + 1) * VB] if g < 3 else high[(g - 3) * VB : (g - 2) * VB]
-            turned[g, at, 256:512] = extra
+    def turn(pair, _):
+        messages = []
+        for k in range(2):
+            message = got_ref[pl.ds(pl.multiple_of((2 * pair + k) * 32, 32), 32)].astype(jnp.float32)
+            messages.append(message.reshape(256, LANE).astype(jnp.bfloat16))
+        both = dot(unit, jnp.concatenate(messages, axis=1), ((1,), (1,)))
+        for k in range(2):
+            rows = both[k * LANE : (k + 1) * LANE]
+            at = pl.ds(pl.multiple_of((2 * pair + k) * VB, VB), VB)
+            low = jnp.where(even, rows[80:128], 0.0).astype(jnp.bfloat16)
+            high = jnp.where(even, 0.0, rows[80:128]).astype(jnp.bfloat16)
+            for g in range(GROUPS):
+                turned[g, at, 0:256] = rows[g * VB : (g + 1) * VB].astype(jnp.bfloat16)
+                extra = low[g * VB : (g + 1) * VB] if g < 3 else high[(g - 3) * VB : (g - 2) * VB]
+                turned[g, at, 256:512] = extra
         return 0
 
-    lax.fori_loop(0, MEM, turn, 0, unroll=True)
+    lax.fori_loop(0, MEM // 2, turn, 0, unroll=True)
 
     first_half = lax.broadcasted_iota(jnp.int32, (8, LANE), 1) < 64
 
@@ -334,6 +349,7 @@
     sent, table = pl.pallas_call(
         forward_kernel,
         in_specs=[vmem_spec, any_spec, any_spec],
+        out_specs=[any_spec, any_spec],
         out_shape=[
             jax.ShapeDtypeStruct((512, 8, LANE), jnp.bfloat16),
             jax.ShapeDtypeStruct((640, NLON), jnp.bfloat16),
@@ -342,7 +358,9 @@
             pltpu.VMEM((1, 12, 64, NLON), jnp.bfloat16),
             pltpu.VMEM((12, 64, NLON), jnp.bfloat16),
             pltpu.VMEM((2, 2048, LANE), jnp.float32),
-            pltpu.SemaphoreType.DMA((2,)),
+            pltpu.VMEM((512, 8, LANE), jnp.bfloat16),
+            pltpu.VMEM((640, NLON), jnp.bfloat16),
+            pltpu.SemaphoreType.DMA((5,)),
         ],
         compiler_params=pltpu.CompilerParams(vmem_limit_bytes=60 * mib),
         cost_estimate=pl.CostEstimate(flops=3 * 10**9, bytes_accessed=4 * 10**6, transcendentals=0),

time: 113 us -> 113 us (level)
  no operation moved by 1% of the time
where the time goes in v5:
time: 113 us
  blocking collectives  42.8 us (38%)
  waiting for transfers between devices  26.7 us (24%)
  starting transfers between devices  22.2 us (20%)
  Pallas kernels  18.8 us (17%)
    all_to_all x1, blocking collectives, body(): got = lax.all_to_all(sent, MESH_AXES, 0, 0, tiled=True)  42.8 us
    all_to_all x1, waiting for transfers between devices, body(): got = lax.all_to_all(sent, MESH_AXES, 0, 0, tiled=True)  26.7 us
    all_to_all x1, starting transfers between devices, body(): got = lax.all_to_all(sent, MESH_AXES, 0, 0, tiled=True)  22.2 us
    pallas_call x1, Pallas kernels, body(): pl.pallas_call(score_kernel, out_shape=jax.ShapeDtypeStruct((512, 8, LANE...  5.85 us
    pallas_call x1, Pallas kernels, body(): pl.pallas_call(forward_kernel, in_specs=[vmem_spec, any_spec, any_spec],...  5.35 us
    pallas_call x1, Pallas kernels, body(): pl.pallas_call(legendre_kernel, out_shape=jax.ShapeDtypeStruct((DEG, 1536...  4.5 us
    pallas_call x1, Pallas kernels, body(): pl.pallas_call(inverse_kernel, in_specs=[vmem_spec, vmem_spec], out_specs...  3.09 us
  transfers between devices with their start and end apart: 1, of which 1 were waited for; matrix products, arithmetic and copies ran while one was open for 1% of the time, Pallas kernels for 4%

profile of v5, /device:TPU:1, one launch (start us, length us, event | category | flops | bytes accessed | tf_op | source)
XLA Modules:
  0.0 113.0 jit_solution(13991083175162246645)
XLA Ops:
  0.6 5.4 %forward.1 = (bf16[512,8,128]{2,1,0:T(8,128)(2,1)}, bf16[640,720]{1,0:T(8,128)(2,1)}) custom-call(s32[320]{0:T(512)} %wave_ref.1, bf16[1,12,64,720]{3,2,1,0:T(8,128)(2,1)} %bitcast.8, bf16[12,64,720]{2,1,0:T(8,128)(2,1)} %bitcast.9), custom_call_target="tpu_custom_call" | custom-call | flops 3000000000 | bytes 4000000 | tf_op jit(solution)/shard_map/forward/pallas_call | solution.py:349
  6.0 0.0 copy-start.4
  6.0 0.0 copy-start
  6.0 0.0 copy-start.1
  6.0 0.0 copy-start.2
  6.0 22.2 %all-to-all-start = ((bf16[512,8,128]{2,1,0:T(8,128)(2,1)}), bf16[512,8,128]{2,1,0:T(8,128)(2,1)S(1)}, u32[]{:S(2)}, u32[]{:S(2)}) async-start(bf16[512,8,128]{2,1,0:T(8,128)(2,1)} %get-tuple-element.6), calls=%async_computation | async-start | bytes 2097152 | tf_op jit(solution)/shard_map/all_to_all | solution.py:369
  28.2 0.0 copy-done.4
  28.3 0.1 dynamic_slice.3
  28.4 0.6 slice.3
  28.9 0.7 multiply_bitcast_fusion
  29.7 0.1 copy.8.wave_ref
  29.7 0.1 copy.9.base_ref
  29.8 0.0 copy-done
  29.8 0.0 copy-done.1
  29.8 0.0 copy-done.2
  29.8 4.5 %legendre.1.leg_ref = bf16[320,1536]{1,0:T(8,128)(2,1)S(1)} custom-call(f32[8,1]{1,0:T(8,128)S(1)} %copy.8.wave_ref, f32[8,1]{1,0:T(8,128)S(1)} %copy.9.base_ref, f32[1,512]{1,0:T(1,128)S(1)} %copy-done, f32[1,512]{1,0:T(1,128)S(1)} %copy-done.1, f32[1,512]{1,0:T(1,128)S(1)} %copy-done.2), custom_call_target="tpu_custom_call" | custom-call | flops 100000000 | bytes 2000000 | tf_op jit(solution)/shard_map/legendre/pallas_call | solution.py:380
  34.3 26.7 %all-to-all-done.got_ref = bf16[512,8,128]{2,1,0:T(8,128)(2,1)S(1)} async-done(((bf16[512,8,128]{2,1,0:T(8,128)(2,1)}), bf16[512,8,128]{2,1,0:T(8,128)(2,1)S(1)}, u32[]{:S(2)}, u32[]{:S(2)}) %all-to-all-start) | async-done | bytes 1048608 | tf_op jit(solution)/shard_map/all_to_all | solution.py:369
  61.1 5.9 %score.1 = bf16[512,8,128]{2,1,0:T(8,128)(2,1)S(1)} custom-call(bf16[512,8,128]{2,1,0:T(8,128)(2,1)S(1)} %all-to-all-done.got_ref, bf16[320,1536]{1,0:T(8,128)(2,1)S(1)} %legendre.1.leg_ref), custom_call_target="tpu_custom_call" | custom-call | flops 6000000000 | bytes 5000000 | tf_op jit(solution)/shard_map/score/pallas_call | solution.py:389
  66.9 0.0 copy-start.3
  66.9 42.8 %all_to_all.10.got_ref = bf16[512,8,128]{2,1,0:T(8,128)(2,1)S(1)} all-to-all(bf16[512,8,128]{2,1,0:T(8,128)(2,1)S(1)} %score.1), channel_id=1, replica_groups=mesh['ens'=16,'lat'=32] {'ens','lat'}, dimensions={0} | all-to-all | bytes 2097152 | tf_op jit(solution)/shard_map/all_to_all | solution.py:402
  109.8 0.0 copy-done.3
  109.8 3.1 %inverse.1 = (bf16[1,12,64,720]{3,2,1,0:T(8,128)(2,1)}, f32[10,20]{1,0:T(8,128)}) custom-call(bf16[512,8,128]{2,1,0:T(8,128)(2,1)S(1)} %all_to_all.10.got_ref, bf16[640,720]{1,0:T(8,128)(2,1)S(1)} %copy-done.3), custom_call_target="tpu_custom_call" | custom-call | flops 2000000000 | bytes 4000000 | tf_op jit(solution)/shard_map/inverse/pallas_call | solution.py:404
  (1 shorter events, 0.0 us)
Async XLA Ops:
  6.0 22.2 %copy-start.4 = (s32[320]{0:T(512)S(1)}, s32[320]{0:T(512)}, u32[]{:S(2)}) copy-start(s32[320]{0:T(512)} %wave_ref.1) | copy-start | bytes 3844
  6.0 23.8 %copy-start = (f32[1,512]{1,0:T(1,128)S(1)}, f32[1,512]{1,0:T(1,128)}, u32[]{:S(2)}) copy-start(f32[1,512]{1,0:T(1,128)} %constant.112.clone.cos_ref) | copy-start | bytes 6148
  6.0 23.8 %copy-start.1 = (f32[1,512]{1,0:T(1,128)S(1)}, f32[1,512]{1,0:T(1,128)}, u32[]{:S(2)}) copy-start(f32[1,512]{1,0:T(1,128)} %constant.113.clone.logsin_ref) | copy-start | bytes 6148
  6.0 23.8 %copy-start.2 = (f32[1,512]{1,0:T(1,128)S(1)}, f32[1,512]{1,0:T(1,128)}, u32[]{:S(2)}) copy-start(f32[1,512]{1,0:T(1,128)} %constant.114.clone.weight_ref) | copy-start | bytes 6148
  6.0 55.0 %all-to-all-start = ((bf16[512,8,128]{2,1,0:T(8,128)(2,1)}), bf16[512,8,128]{2,1,0:T(8,128)(2,1)S(1)}, u32[]{:S(2)}, u32[]{:S(2)}) async-start(bf16[512,8,128]{2,1,0:T(8,128)(2,1)} %get-tuple-element.6), calls=%async_computation | async-start | bytes 2097152 | tf_op jit(solution)/shard_map/all_to_all | solution.py:369
  66.9 42.9 %copy-start.3 = (bf16[640,720]{1,0:T(8,128)(2,1)S(1)}, bf16[640,720]{1,0:T(8,128)(2,1)}, u32[]{:S(2)}) copy-start(bf16[640,720]{1,0:T(8,128)(2,1)} %get-tuple-element.7.table_ref) | copy-start | bytes 2764804

commit v6 on v5

--- a/solution.py
+++ b/solution.py
@@ -292,23 +292,19 @@
     for t in range(4):
         pair = [rows[pl.ds(2 * t + c, 512, stride=8), :].astype(jnp.bfloat16) for c in range(2)]
         turned.append(dot(order, jnp.concatenate(pair, axis=1), ((1,), (1,))).astype(jnp.bfloat16))
+    left = []
+    for vb in range(4):
+        for t in range(4):
+            tiles = [turned[t][g * 48 : (g + 1) * 48, vb * LANE : (vb + 1) * LANE] for g in range(GROUPS)]
+            left.append(jnp.concatenate(tiles, axis=1))
+    result = dot(jnp.concatenate(left, axis=0), table_ref[...]).astype(jnp.bfloat16)
     stores = []
     for h in range(2):
-        left = []
         for vb in (2 * h, 2 * h + 1):
-            for t in range(4):
-                left.append(
-                    jnp.concatenate(
-                        [turned[t][g * 48 : (g + 1) * 48, vb * LANE : (vb + 1) * LANE] for g in range(GROUPS)],
-                        axis=1,
-                    )
-                )
-        result = dot(jnp.concatenate(left, axis=0), table_ref[...]).astype(jnp.bfloat16)
-        for vb in range(2):
             for t in range(4):
                 for k, j in enumerate((2 * t, 2 * t + 1, 8 + t)):
                     at = (vb * 4 + t) * 48 + k * VB
-                    grid[0, j, h * 32 + vb * VB : h * 32 + (vb + 1) * VB, :] = result[at : at + VB]
+                    grid[0, j, vb * VB : (vb + 1) * VB, :] = result[at : at + VB]
         half = (slice(None), slice(None), slice(h * 32, (h + 1) * 32), slice(None))
         stores.append(pltpu.make_async_copy(grid.at[half], grid_hbm.at[half], sems.at[h]))
         stores[-1].start()

time: 113 us -> 113 us (level)
  no operation moved by 1% of the time
where the time goes in v6:
time: 113 us
  blocking collectives  42.8 us (38%)
  waiting for transfers between devices  26.7 us (24%)
  starting transfers between devices  22.2 us (20%)
  Pallas kernels  19 us (17%)
    all_to_all x1, blocking collectives, body(): got = lax.all_to_all(sent, MESH_AXES, 0, 0, tiled=True)  42.8 us
    all_to_all x1, waiting for transfers between devices, body(): got = lax.all_to_all(sent, MESH_AXES, 0, 0, tiled=True)  26.7 us
    all_to_all x1, starting transfers between devices, body(): got = lax.all_to_all(sent, MESH_AXES, 0, 0, tiled=True)  22.2 us
    pallas_call x1, Pallas kernels, body(): pl.pallas_call(score_kernel, out_shape=jax.ShapeDtypeStruct((512, 8, LANE...  5.85 us
    pallas_call x1, Pallas kernels, body(): pl.pallas_call(forward_kernel, in_specs=[vmem_spec, any_spec, any_spec],...  5.35 us
    pallas_call x1, Pallas kernels, body(): pl.pallas_call(legendre_kernel, out_shape=jax.ShapeDtypeStruct((DEG, 1536...  4.5 us
    pallas_call x1, Pallas kernels, body(): pl.pallas_call(inverse_kernel, in_specs=[vmem_spec, vmem_spec], out_specs...  3.3 us
  transfers between devices with their start and end apart: 1, of which 1 were waited for; matrix products, arithmetic and copies ran while one was open for 1% of the time, Pallas kernels for 4%

profile of v6, /device:TPU:1, one launch (start us, length us, event | category | flops | bytes accessed | tf_op | source)
XLA Modules:
  0.0 113.2 jit_solution(6351458977050622153)
XLA Ops:
  0.6 5.4 %forward.1 = (bf16[512,8,128]{2,1,0:T(8,128)(2,1)}, bf16[640,720]{1,0:T(8,128)(2,1)}) custom-call(s32[320]{0:T(512)} %wave_ref.1, bf16[1,12,64,720]{3,2,1,0:T(8,128)(2,1)} %bitcast.8, bf16[12,64,720]{2,1,0:T(8,128)(2,1)} %bitcast.9), custom_call_target="tpu_custom_call" | custom-call | flops 3000000000 | bytes 4000000 | tf_op jit(solution)/shard_map/forward/pallas_call | solution.py:345
  6.0 0.0 copy-start.4
  6.0 0.0 copy-start
  6.0 0.0 copy-start.1
  6.0 0.0 copy-start.2
  6.0 22.2 %all-to-all-start = ((bf16[512,8,128]{2,1,0:T(8,128)(2,1)}), bf16[512,8,128]{2,1,0:T(8,128)(2,1)S(1)}, u32[]{:S(2)}, u32[]{:S(2)}) async-start(bf16[512,8,128]{2,1,0:T(8,128)(2,1)} %get-tuple-element.6), calls=%async_computation | async-start | bytes 2097152 | tf_op jit(solution)/shard_map/all_to_all | solution.py:365
  28.2 0.0 copy-done.4
  28.3 0.1 dynamic_slice.3
  28.4 0.6 slice.3
  28.9 0.7 multiply_bitcast_fusion
  29.7 0.1 copy.8.wave_ref
  29.7 0.1 copy.9.base_ref
  29.8 0.0 copy-done
  29.8 0.0 copy-done.1
  29.8 0.0 copy-done.2
  29.8 4.5 %legendre.1.leg_ref = bf16[320,1536]{1,0:T(8,128)(2,1)S(1)} custom-call(f32[8,1]{1,0:T(8,128)S(1)} %copy.8.wave_ref, f32[8,1]{1,0:T(8,128)S(1)} %copy.9.base_ref, f32[1,512]{1,0:T(1,128)S(1)} %copy-done, f32[1,512]{1,0:T(1,128)S(1)} %copy-done.1, f32[1,512]{1,0:T(1,128)S(1)} %copy-done.2), custom_call_target="tpu_custom_call" | custom-call | flops 100000000 | bytes 2000000 | tf_op jit(solution)/shard_map/legendre/pallas_call | solution.py:376
  34.3 26.7 %all-to-all-done.got_ref = bf16[512,8,128]{2,1,0:T(8,128)(2,1)S(1)} async-done(((bf16[512,8,128]{2,1,0:T(8,128)(2,1)}), bf16[512,8,128]{2,1,0:T(8,128)(2,1)S(1)}, u32[]{:S(2)}, u32[]{:S(2)}) %all-to-all-start) | async-done | bytes 1048608 | tf_op jit(solution)/shard_map/all_to_all | solution.py:365
  61.1 5.9 %score.1 = bf16[512,8,128]{2,1,0:T(8,128)(2,1)S(1)} custom-call(bf16[512,8,128]{2,1,0:T(8,128)(2,1)S(1)} %all-to-all-done.got_ref, bf16[320,1536]{1,0:T(8,128)(2,1)S(1)} %legendre.1.leg_ref), custom_call_target="tpu_custom_call" | custom-call | flops 6000000000 | bytes 5000000 | tf_op jit(solution)/shard_map/score/pallas_call | solution.py:385
  66.9 0.0 copy-start.3
  66.9 42.8 %all_to_all.10.got_ref = bf16[512,8,128]{2,1,0:T(8,128)(2,1)S(1)} all-to-all(bf16[512,8,128]{2,1,0:T(8,128)(2,1)S(1)} %score.1), channel_id=1, replica_groups=mesh['ens'=16,'lat'=32] {'ens','lat'}, dimensions={0} | all-to-all | bytes 2097152 | tf_op jit(solution)/shard_map/all_to_all | solution.py:398
  109.8 0.0 copy-done.3
  109.8 3.3 %inverse.1 = (bf16[1,12,64,720]{3,2,1,0:T(8,128)(2,1)}, f32[10,20]{1,0:T(8,128)}) custom-call(bf16[512,8,128]{2,1,0:T(8,128)(2,1)S(1)} %all_to_all.10.got_ref, bf16[640,720]{1,0:T(8,128)(2,1)S(1)} %copy-done.3), custom_call_target="tpu_custom_call" | custom-call | flops 2000000000 | bytes 4000000 | tf_op jit(solution)/shard_map/inverse/pallas_call | solution.py:400
  (1 shorter events, 0.0 us)
Async XLA Ops:
  6.0 22.2 %copy-start.4 = (s32[320]{0:T(512)S(1)}, s32[320]{0:T(512)}, u32[]{:S(2)}) copy-start(s32[320]{0:T(512)} %wave_ref.1) | copy-start | bytes 3844
  6.0 23.8 %copy-start = (f32[1,512]{1,0:T(1,128)S(1)}, f32[1,512]{1,0:T(1,128)}, u32[]{:S(2)}) copy-start(f32[1,512]{1,0:T(1,128)} %constant.112.clone.cos_ref) | copy-start | bytes 6148
  6.0 23.8 %copy-start.1 = (f32[1,512]{1,0:T(1,128)S(1)}, f32[1,512]{1,0:T(1,128)}, u32[]{:S(2)}) copy-start(f32[1,512]{1,0:T(1,128)} %constant.113.clone.logsin_ref) | copy-start | bytes 6148
  6.0 23.8 %copy-start.2 = (f32[1,512]{1,0:T(1,128)S(1)}, f32[1,512]{1,0:T(1,128)}, u32[]{:S(2)}) copy-start(f32[1,512]{1,0:T(1,128)} %constant.114.clone.weight_ref) | copy-start | bytes 6148
  6.0 55.0 %all-to-all-start = ((bf16[512,8,128]{2,1,0:T(8,128)(2,1)}), bf16[512,8,128]{2,1,0:T(8,128)(2,1)S(1)}, u32[]{:S(2)}, u32[]{:S(2)}) async-start(bf16[512,8,128]{2,1,0:T(8,128)(2,1)} %get-tuple-element.6), calls=%async_computation | async-start | bytes 2097152 | tf_op jit(solution)/shard_map/all_to_all | solution.py:365
  66.9 42.9 %copy-start.3 = (bf16[640,720]{1,0:T(8,128)(2,1)S(1)}, bf16[640,720]{1,0:T(8,128)(2,1)}, u32[]{:S(2)}) copy-start(bf16[640,720]{1,0:T(8,128)(2,1)} %get-tuple-element.7.table_ref) | copy-start | bytes 2764804
